TPU v7x, 128 devices: a whole 4x4x4 slice. The times are simulated.
128 devices in a mesh: tok: 16 (over y, z), exp: 8 (over x, core).
Axes of the slice: x: 4, y: 4, z: 4, core: 2. Of those that a mesh axis runs over, the one named last changes fastest.
Arguments:
- activations: bfloat16 [16384, 6144], P(('tok', 'exp')), may hold values from -6 to 6
- expert_ids: int32 [16384, 2], P(('tok', 'exp')), may hold values from 0 to 7, all different within a row; in each aligned block of 128 rows (0 to 127, 128 to 255, ...) at most 48 rows name the same one
- out_grads: bfloat16 [16384, 2, 16384], P(('tok', 'exp')), may hold values from -6 to 6
- sketch_matrix: bfloat16 [8, 16384, 128], P('exp'), may hold values from -0.046875 to 0.046875
Outputs:
- projector: float32 [8, 6144, 128], P('exp', 'tok')
Inputs may be any that keep to these rules, and one draw needn't show every extreme that they name: `expert_ids`: each token names 2 different experts. In the tokens of one device (aligned blocks of 128 rows) no expert is named by more than 48 tokens, a bound that some block reaches.
All inputs are finite; a program needn't handle non-finite values.
Results may differ from a plain program's by a relative error of at most 0.034.
Values may be sent and summed in bfloat16 or wider, within the bound.
A program may use at most 128 MiB of HBM per device.

v0:
```python
import jax
import jax.numpy as jnp
from jax import lax
from jax.sharding import PartitionSpec as P

D = 6144


HIGH = lax.Precision.HIGHEST


def orthonormal(block):
    gram = jnp.einsum(
        "erk,erl->ekl", block, block, precision=HIGH, preferred_element_type=jnp.float32
    )
    gram = lax.psum(gram.astype(jnp.bfloat16), "tok").astype(jnp.float32)
    lower = jnp.linalg.cholesky(gram)
    return lax.linalg.triangular_solve(lower, block, left_side=False, lower=True, transpose_a=True)


def shards(activations, expert_ids, out_grads, sketch_matrix):
    tok_rows = activations.shape[0]
    width = activations.shape[1]
    top_count = expert_ids.shape[1]
    hidden = out_grads.shape[2]
    local_experts = sketch_matrix.shape[0]
    owners = lax.axis_size("exp")
    n_experts = local_experts * owners
    capacity = tok_rows * top_count * 3 // (2 * n_experts)
    pairs = tok_rows * top_count
    flat_ids = expert_ids.reshape(pairs)
    onehot = (flat_ids[:, None] == jnp.arange(n_experts, dtype=jnp.int32)[None, :]).astype(
        jnp.int32
    )
    before = jnp.cumsum(onehot, axis=0) - onehot
    ranks = jnp.sum(before * onehot, axis=1)
    slots = flat_ids * capacity + ranks
    source = (
        jnp.zeros((n_experts * capacity,), jnp.int32)
        .at[slots]
        .set(jnp.arange(pairs, dtype=jnp.int32) + 1)
    )
    filled = (source > 0)[:, None]
    pair_index = jnp.maximum(source - 1, 0)
    token_index = pair_index // top_count
    slices = lax.axis_size("tok")
    col_width = width // slices
    col_hidden = hidden // slices
    tok_place = lax.axis_index("tok")
    act_split = activations.reshape(tok_rows, slices, col_width).transpose(1, 0, 2)
    grad_split = out_grads.reshape(pairs, slices, col_hidden).transpose(1, 0, 2)
    send_x = jnp.where(filled[None], act_split[:, token_index], 0)
    send_g = jnp.where(filled[None], grad_split[:, pair_index], 0)
    send_x = send_x.reshape(slices * owners, local_experts * capacity, col_width)
    send_g = send_g.reshape(slices * owners, local_experts * capacity, col_hidden)
    recv_x, recv_g = (
        lax.all_to_all(send_x, ("tok", "exp"), split_axis=0, concat_axis=0, tiled=True),
        lax.all_to_all(send_g, ("tok", "exp"), split_axis=0, concat_axis=0, tiled=True),
    )
    senders = slices * owners
    cols_x = (
        recv_x.reshape(senders, local_experts, capacity, col_width)
        .transpose(1, 0, 2, 3)
        .reshape(local_experts, senders * capacity, col_width)
    )
    cols_g = (
        recv_g.reshape(senders, local_experts, capacity, col_hidden)
        .transpose(1, 0, 2, 3)
        .reshape(local_experts, senders * capacity, col_hidden)
    )
    omega_rows = lax.dynamic_slice_in_dim(sketch_matrix, tok_place * col_hidden, col_hidden, 1)
    proj_part = jnp.einsum("emf,efr->emr", cols_g, omega_rows, preferred_element_type=jnp.float32)
    proj = lax.psum(proj_part, "tok").astype(jnp.bfloat16)
    sketch_rows = jnp.einsum("emd,emr->edr", cols_x, proj, preferred_element_type=jnp.float32)
    basis_rows = orthonormal(sketch_rows).astype(jnp.bfloat16)
    weight_part = jnp.einsum("emd,edr->emr", cols_x, basis_rows, preferred_element_type=jnp.float32)
    weights = lax.psum(weight_part.astype(jnp.bfloat16), "tok")
    power_rows = jnp.einsum("emf,emr->efr", cols_g, weights, preferred_element_type=jnp.float32)
    right_rows = orthonormal(power_rows).astype(jnp.bfloat16)
    second_part = jnp.einsum("emf,efr->emr", cols_g, right_rows, preferred_element_type=jnp.float32)
    second = lax.psum(second_part.astype(jnp.bfloat16), "tok")
    refined_rows = jnp.einsum("emd,emr->edr", cols_x, second, preferred_element_type=jnp.float32)
    return orthonormal(refined_rows) * jnp.float32(D**0.5)


def solution(mesh):
    return jax.shard_map(
        shards,
        mesh=mesh,
        in_specs=(
            P(("tok", "exp"), None),
            P(("tok", "exp"), None),
            P(("tok", "exp"), None, None),
            P("exp", None, None),
        ),
        out_specs=P("exp", "tok", None),
        check_vma=False,
    )
```

profile of v0, /device:TPU:0, one launch (start us, length us, event | category | flops | bytes accessed | tf_op | source)
XLA Modules:
  0.0 893.2 jit_solution(1565931982866859417)
XLA Ops:
  6.5 0.8 copy.23
  7.3 0.1 eq.29
  7.5 0.1 eq.25
  7.6 0.7 broadcast_multiply_fusion
  8.3 0.6 reduce-window.6
  8.9 0.2 slice_reduce_fusion
  9.1 0.1 copy.22
  9.2 0.1 mul.30
  9.4 0.1 fusion.25
  9.5 1.4 scatter_custom_fusion
  10.9 14.5 %reshape.214 = bf16[256,16,1024]{2,1,0:T(8,128)(2,1)} reshape(bf16[128,2,16384]{2,1,0:T(2,128)(2,1)} %param.9) | data formatting | bytes 16777216 | tf_op jit(solution)/shard_map/reshape | solution.py:51
  25.4 14.7 %gather_fusion.1 = bf16[384,16,1024]{2,1,0:T(8,128)(2,1)} fusion(bf16[16,256,1024]{2,0,1:T(8,128)(2,1)} %bitcast.101, s32[1024]{0:T(1024)S(1)} %get-tuple-element.9), kind=kCustom, calls=%fused_computation.1 | custom fusion | bytes 25167360 | tf_op jit(solution)/shard_map/gather | solution.py:53
  40.1 14.6 %copy.26 = bf16[16,384,1024]{2,1,0:T(8,128)(2,1)} copy(bf16[16,384,1024]{2,0,1:T(8,128)(2,1)} %bitcast.102) | data formatting | bytes 25165824 | tf_op jit(solution)/shard_map/gather | solution.py:53
  54.6 0.1 broadcast_in_dim.40
  54.7 10.7 %broadcast_select_fusion = bf16[128,48,1024]{2,1,0:T(8,128)(2,1)} fusion(bf16[128,48,1024]{2,1,0:T(8,128)(2,1)} %bitcast.103, pred[128,48]{1,0:T(8,128)(4,1)S(1)} %broadcast_bitcast_fusion), kind=kLoop, calls=%fused_computation.3 | loop fusion | flops 6291456 | bytes 25171968 | tf_op jit(solution)/shard_map/jit(_where)/select_n | solution.py:53
  65.4 0.0 copy-start
  65.4 11.6 %all-to-all-start.1 = ((bf16[128,48,1024]{2,1,0:T(8,128)(2,1)}), bf16[128,48,1024]{2,1,0:T(8,128)(2,1)}, u32[]{:S(2)}, u32[]{:S(2)}) async-start(bf16[128,48,1024]{2,1,0:T(8,128)(2,1)} %broadcast_select_fusion), calls=%async_computation.1 | async-start | bytes 25165824 | tf_op jit(solution)/shard_map/all_to_all | solution.py:58
  77.0 0.0 copy-done
  77.0 0.3 copy.37
  77.3 3.9 gather_fusion
  81.3 3.5 copy.25
  84.7 3.1 broadcast_select_fusion.1
  87.9 149.9 %all-to-all-done.1 = bf16[128,48,1024]{2,1,0:T(8,128)(2,1)} async-done(((bf16[128,48,1024]{2,1,0:T(8,128)(2,1)}), bf16[128,48,1024]{2,1,0:T(8,128)(2,1)}, u32[]{:S(2)}, u32[]{:S(2)}) %all-to-all-start.1) | async-done | bytes 12582944 | tf_op jit(solution)/shard_map/all_to_all | solution.py:58
  237.8 15.8 %all-to-all-start = ((bf16[128,48,384]{2,1,0:T(8,128)(2,1)}), bf16[128,48,384]{2,1,0:T(8,128)(2,1)}, u32[]{:S(2)}, u32[]{:S(2)}) async-start(bf16[128,48,384]{2,1,0:T(8,128)(2,1)} %broadcast_select_fusion.1), calls=%async_computation | async-start | bytes 9437184 | tf_op jit(solution)/shard_map/all_to_all | solution.py:57
  253.6 0.2 all-reduce.4.cloned.1.call-start
  253.8 6.5 convolution_bitcast_fusion
  260.3 133.8 %all-reduce.7 = bf16[1,6144,128]{2,1,0:T(8,128)(2,1)} all-reduce(f32[1,6144,128]{2,1,0:T(8,128)S(1)} %convolution_bitcast_fusion), channel_id=1, replica_groups=mesh['tok'=16,'exp'=8] {'tok'}, use_global_device_ids=true, to_apply=%region_4.5 | all-reduce | flops 786432 | bytes 4718592 | tf_op jit(solution)/shard_map/psum | solution.py:73
  394.1 0.0 all-to-all-done
  394.1 4.2 fusion
  398.4 0.5 fusion.7
  398.9 73.1 %psum.43 = bf16[1,128,128]{1,2,0:T(8,128)(2,1)S(1)} all-reduce(bf16[1,128,128]{1,2,0:T(8,128)(2,1)S(1)} %fusion.7), channel_id=1, replica_groups=mesh['tok'=16,'exp'=8] {'tok'}, use_global_device_ids=true, to_apply=%region_5.6 | all-reduce | flops 16384 | bytes 65536 | tf_op jit(solution)/shard_map/psum | solution.py:16
  472.0 0.1 copy.28
  472.1 11.7 %custom-call.13 = f32[1,128,128]{2,1,0:T(8,128)S(1)} custom-call(f32[1,128,128]{2,1,0:T(8,128)S(1)} %fusion.19), custom_call_target="Cholesky" | custom-call | tf_op jit(solution)/shard_map/jit(cholesky)/cholesky | solution.py:17
  483.9 0.6 compare_reduce_fusion.2
  484.5 0.7 fusion.11
  485.2 9.8 %custom-call.14 = f32[1,1,128,128]{2,3,1,0:T(8,128)S(1)} custom-call(f32[1,1,128,128]{3,2,1,0:T(8,128)S(1)} %fusion.11), custom_call_target="InvertDiagBlocksLowerTriangular" | custom-call | tf_op jit(solution)/shard_map/triangular_solve/custom-call.0 | solution.py:18
  495.0 0.4 fusion.5
  495.4 4.9 convolution_convert_fusion
  500.3 0.0 all-reduce.4.cloned.1.call-update
  500.3 0.0 all-reduce.6.cloned.1.call-start
  500.4 85.7 %all-reduce.4.cloned.1.call-done = bf16[6144,128]{1,0:T(8,128)(2,1)} async-done(((bf16[6144,128]{1,0:T(8,128)(2,1)}), bf16[6144,128]{1,0:T(8,128)(2,1)}) %all-reduce.4.cloned.1.call-update) | async-done | bytes 1572880 | tf_op jit(solution)/shard_map/psum | solution.py:77
  586.1 6.9 fusion.31
  593.0 1.0 fusion.6
  594.0 72.4 %psum.45 = bf16[1,128,128]{1,2,0:T(8,128)(2,1)S(1)} all-reduce(bf16[1,128,128]{1,2,0:T(8,128)(2,1)S(1)} %fusion.6), channel_id=1, replica_groups=mesh['tok'=16,'exp'=8] {'tok'}, use_global_device_ids=true, to_apply=%region_9.12 | all-reduce | flops 16384 | bytes 65536 | tf_op jit(solution)/shard_map/psum | solution.py:16
  666.4 0.1 copy.30
  666.5 11.7 %custom-call.15 = f32[1,128,128]{2,1,0:T(8,128)S(1)} custom-call(f32[1,128,128]{2,1,0:T(8,128)S(1)} %fusion.17), custom_call_target="Cholesky" | custom-call | tf_op jit(solution)/shard_map/jit(cholesky)/cholesky | solution.py:17
  678.3 0.6 compare_reduce_fusion.1
  678.9 0.7 fusion.12
  679.6 9.8 %custom-call.9 = f32[1,1,128,128]{2,3,1,0:T(8,128)S(1)} custom-call(f32[1,1,128,128]{3,2,1,0:T(8,128)S(1)} %fusion.12), custom_call_target="InvertDiagBlocksLowerTriangular" | custom-call | tf_op jit(solution)/shard_map/triangular_solve | solution.py:18
  689.4 0.6 convolution_convert_fusion.2
  690.0 9.2 %convolution_convert_fusion.1 = bf16[6144,128]{1,0:T(8,128)(2,1)} fusion(bf16[6144,1024]{1,0:T(8,128)(2,1)} %bitcast.12, bf16[1024,128]{1,0:T(8,128)(2,1)S(1)} %convolution_convert_fusion.2), kind=kOutput, calls=%fused_computation.6 | convolution fusion | flops 1611399168 | bytes 14417920 | tf_op jit(solution)/shard_map/emf,efr->emr/dot_general | solution.py:80
  699.2 0.0 all-reduce.6.cloned.1.call-update
  699.2 85.3 %all-reduce.6.cloned.1.call-done = bf16[6144,128]{1,0:T(8,128)(2,1)} async-done(((bf16[6144,128]{1,0:T(8,128)(2,1)}), bf16[6144,128]{1,0:T(8,128)(2,1)}) %all-reduce.6.cloned.1.call-update) | async-done | bytes 1572880 | tf_op jit(solution)/shard_map/psum | solution.py:81
  784.5 4.2 fusion.32
  788.7 0.5 fusion.8
  789.2 72.4 %psum.47 = bf16[1,128,128]{1,2,0:T(8,128)(2,1)S(1)} all-reduce(bf16[1,128,128]{1,2,0:T(8,128)(2,1)S(1)} %fusion.8), channel_id=1, replica_groups=mesh['tok'=16,'exp'=8] {'tok'}, use_global_device_ids=true, to_apply=%region_11.14 | all-reduce | flops 16384 | bytes 65536 | tf_op jit(solution)/shard_map/psum | solution.py:16
  861.7 0.1 copy.32
  861.8 11.7 %custom-call.16 = f32[1,128,128]{2,1,0:T(8,128)S(1)} custom-call(f32[1,128,128]{2,1,0:T(8,128)S(1)} %fusion.15), custom_call_target="Cholesky" | custom-call | tf_op jit(solution)/shard_map/jit(cholesky)/cholesky | solution.py:17
  873.5 0.6 compare_reduce_fusion
  874.2 0.7 fusion.13
  874.8 9.8 %custom-call.17 = f32[1,1,128,128]{2,3,1,0:T(8,128)S(1)} custom-call(f32[1,1,128,128]{3,2,1,0:T(8,128)S(1)} %fusion.13), custom_call_target="InvertDiagBlocksLowerTriangular" | custom-call | tf_op jit(solution)/shard_map/triangular_solve/custom-call.0 | solution.py:18
  884.7 0.4 fusion.3
  885.1 0.8 copy.33
  (15 shorter events, 0.2 us)
Async XLA Ops:
  65.4 11.6 %copy-start = (bf16[128,6144]{1,0:T(8,128)(2,1)S(1)}, bf16[128,6144]{1,0:T(8,128)(2,1)}, u32[]{:S(2)}) copy-start(bf16[128,6144]{1,0:T(8,128)(2,1)} %param.7) | copy-start | bytes 4718596
  65.4 172.4 %all-to-all-start.1 = ((bf16[128,48,1024]{2,1,0:T(8,128)(2,1)}), bf16[128,48,1024]{2,1,0:T(8,128)(2,1)}, u32[]{:S(2)}, u32[]{:S(2)}) async-start(bf16[128,48,1024]{2,1,0:T(8,128)(2,1)} %broadcast_select_fusion), calls=%async_computation.1 | async-start | bytes 25165824 | tf_op jit(solution)/shard_map/all_to_all | solution.py:58
  237.8 156.3 %all-to-all-start = ((bf16[128,48,384]{2,1,0:T(8,128)(2,1)}), bf16[128,48,384]{2,1,0:T(8,128)(2,1)}, u32[]{:S(2)}, u32[]{:S(2)}) async-start(bf16[128,48,384]{2,1,0:T(8,128)(2,1)} %broadcast_select_fusion.1), calls=%async_computation | async-start | bytes 9437184 | tf_op jit(solution)/shard_map/all_to_all | solution.py:57
  253.6 332.5 %all-reduce.4.cloned.1.call-start = ((), (), s32[]{:S(2)}) async-start(), calls=%async_computation.2 | async-start | bytes 3145728 | tf_op jit(solution)/shard_map/psum | solution.py:77
  500.3 284.2 %all-reduce.6.cloned.1.call-start = ((), (), s32[]{:S(2)}) async-start(), calls=%async_computation.3 | async-start | bytes 3145728 | tf_op jit(solution)/shard_map/psum | solution.py:81
Sparse Core Ops, SparseCore 0:
  500.4 85.5 all-reduce.3
  699.3 85.1 all-reduce.5
where the time goes:
time: 902 us; the launch traced here: 893 us
  blocking collectives  352 us (39%)
  waiting for transfers between devices  321 us (36%)
  other arithmetic  83.8 us (9%)
  local copies, waits for them, and re-layouts  55.5 us (6%)
  matrix products  39.4 us (4%)
  starting transfers between devices  27.6 us (3%)
  between operations  14.1 us (2%)
    psum x3, blocking collectives, orthonormal(): gram = lax.psum(gram.astype(jnp.bfloat16), 'tok').astype(jnp.float32)  218 us
    all_to_all x1, waiting for transfers between devices, shards(): lax.all_to_all(send_g, ('tok', 'exp'), split_axis=0, concat_axis=0, tiled...  150 us
    psum x1, blocking collectives, shards(): proj = lax.psum(proj_part, 'tok').astype(jnp.bfloat16)  134 us
    psum x1, waiting for transfers between devices, shards(): weights = lax.psum(weight_part.astype(jnp.bfloat16), 'tok')  85.7 us
    psum x1, waiting for transfers between devices, shards(): second = lax.psum(second_part.astype(jnp.bfloat16), 'tok')  85.3 us
    another operation x9, other arithmetic, orthonormal(): lower = jnp.linalg.cholesky(gram)  37.2 us
    another operation x6, other arithmetic, orthonormal(): lax.linalg.triangular_solve(lower, block, left_side=False, lower=True, tr...  31.4 us
    gather x2, local copies, waits for them, and re-layouts, shards(): send_g = jnp.where(filled[None], grad_split[:, pair_index], 0)  29.2 us
  transfers between devices with their start and end apart: 4, of which 3 were waited for; matrix products, arithmetic and copies ran while one was open for 2% of the time, Pallas kernels for 0%

commit v1 on v0

v1 whole, which is shorter than its diff:
```python
import functools

import jax
import jax.numpy as jnp
from jax import lax
from jax.experimental import pallas as pl
from jax.experimental.pallas import tpu as pltpu
from jax.sharding import PartitionSpec as P

MESH = pl.DeviceIdType.MESH
HIGH = lax.Precision.HIGHEST
F32 = jnp.float32
BF16 = jnp.bfloat16

N = 4
TOK = N * N
EXP = 2 * N
CAP = 48
ROWS = EXP * CAP
PIECE = 2 * CAP
RANK = 128
PANEL = 16


def dot(a, b):
    return jnp.dot(a, b, preferred_element_type=F32)


def dot_t(a, b, precision=None):
    return lax.dot_general(
        a, b, (((1,), (1,)), ((), ())), precision=precision, preferred_element_type=F32
    )


def sort_kernel(row_ids, col_ids, g_ref, x_ref, gs_ref, xs_ref, pick):
    pairs = row_ids.shape[1]
    toks = x_ref.shape[0]

    @pl.when(pl.program_id(0) == 0)
    def _():
        ids = row_ids[...]
        same = (col_ids[...] == ids) & (
            lax.broadcasted_iota(jnp.int32, (pairs, pairs), 0)
            < lax.broadcasted_iota(jnp.int32, (pairs, pairs), 1)
        )
        rank = jnp.sum(same.astype(F32), axis=0, keepdims=True).astype(jnp.int32)
        slot = ids * CAP + rank
        hot = lax.broadcasted_iota(jnp.int32, (ROWS, pairs), 0) == slot
        pick[...] = hot.astype(F32).astype(BF16)

    first = pick[:, :toks]
    second = pick[:, toks:]
    gs = dot(first, g_ref[:, 0, :]) + dot(second, g_ref[:, 1, :])
    gs_ref[...] = gs.astype(BF16)
    xs_ref[...] = dot(first + second, x_ref[...]).astype(BF16)


def sort_rows(expert_ids, out_grads, activations, steps=16):
    toks, top = expert_ids.shape
    hidden = out_grads.shape[2]
    width = activations.shape[1]
    ids = expert_ids.T.reshape(1, toks * top)
    hc, wc = hidden // steps, width // steps
    return pl.pallas_call(
        sort_kernel,
        grid=(steps,),
        out_shape=(
            jax.ShapeDtypeStruct((ROWS, hidden), BF16),
            jax.ShapeDtypeStruct((ROWS, width), BF16),
        ),
        in_specs=[
            pl.BlockSpec((1, toks * top), lambda i: (0, 0)),
            pl.BlockSpec((toks * top, 1), lambda i: (0, 0)),
            pl.BlockSpec((toks, top, hc), lambda i: (0, 0, i)),
            pl.BlockSpec((toks, wc), lambda i: (0, i)),
        ],
        out_specs=(
            pl.BlockSpec((ROWS, hc), lambda i: (0, i)),
            pl.BlockSpec((ROWS, wc), lambda i: (0, i)),
        ),
        scratch_shapes=[pltpu.VMEM((ROWS, toks * top), BF16)],
        compiler_params=pltpu.CompilerParams(vmem_limit_bytes=40 * 1024 * 1024),
        name="sort",
    )(ids, ids.reshape(toks * top, 1), out_grads, activations)


def bytes_wait(ref, sem):
    pltpu.make_async_copy(ref, ref, sem).wait()


def inverse_factor(c, cm, mm):
    cm[...] = c
    rows = lax.broadcasted_iota(jnp.int32, (RANK, RANK), 0)
    cols = lax.broadcasted_iota(jnp.int32, (RANK, RANK), 1)
    mm[...] = (rows == cols).astype(F32)
    prow = lax.broadcasted_iota(jnp.int32, (PANEL, RANK), 0)
    pcol = lax.broadcasted_iota(jnp.int32, (PANEL, RANK), 1)
    srow = lax.broadcasted_iota(jnp.int32, (PANEL, 1), 0)

    def panel(p, carry):
        base = pl.multiple_of(p * PANEL, PANEL)
        a = pltpu.roll(cm[pl.ds(base, PANEL), :], lax.rem(RANK - base, RANK), 1)
        m = mm[pl.ds(base, PANEL), :]
        for i in range(PANEL):
            ra = a[i : i + 1, :]
            rm = m[i : i + 1, :]
            r = lax.rsqrt(a[i : i + 1, i : i + 1])
            col = jnp.where(srow > i, a[:, i : i + 1] * (r * r), 0.0)
            a = jnp.where(prow == i, a * r, a - col * ra)
            m = jnp.where(prow == i, m * r, m - col * rm)
        mm[pl.ds(base, PANEL), :] = m
        a = pltpu.roll(a, base, 1)
        left = jnp.where(pcol >= base + PANEL, a, 0.0)
        both = jnp.concatenate([a, m], axis=1)
        change = lax.dot_general(
            left, both, (((0,), (0,)), ((), ())), precision=HIGH, preferred_element_type=F32
        )
        cm[...] -= change[:, :RANK]
        mm[...] -= change[:, RANK:]
        return carry

    lax.fori_loop(0, RANK // PANEL, panel, 0)
    return mm[...]


def body(
    scale,
    gs, xs, om,
    out,
    xr, gl, gr, wl, wr,
    nls, nrs, pxl, pxr, pxl2, pxr2,
    sp, rb, rb3, bt,
    ws, wgl, wgr,
    pwl, pwr, rl, rr, rbl, rbr,
    gm, gb, cm, mm,
    ssem, rsem, gsem, selfsem,
):
    tok = lax.axis_index("tok")
    ex = lax.axis_index("exp")
    y, z = lax.div(tok, N), lax.rem(tok, N)
    x, k = lax.div(ex, 2), lax.rem(ex, 2)
    half = gl.shape[1]
    width = xr.shape[1]
    wc = width // TOK
    hc = half // TOK

    def dev(a, b, c, core):
        return (b * N + c, a * 2 + core)

    def add(a, b, n):
        return lax.rem(a + b, n)

    def remote(src, dst, s, r, where):
        return pltpu.make_async_remote_copy(
            src_ref=src, dst_ref=dst, send_sem=s, recv_sem=r, device_id=where, device_id_type=MESH
        )

    def loop(lo, hi, fn):
        lax.fori_loop(lo, hi, lambda i, c: (fn(i), c)[1], 0)

    barrier = pltpu.get_barrier_semaphore()

    def greet(where):
        pl.semaphore_signal(barrier, inc=1, device_id=where, device_id_type=MESH)

    chip = x * TOK + tok

    def same_core(d):
        c = add(chip, d, N * TOK)
        greet((lax.rem(c, TOK), lax.div(c, TOK) * 2 + k))

    loop(1, N * TOK, same_core)

    def other_core(d):
        greet(dev(add(x, d, N), y, z, 1 - k))

    loop(0, N, other_core)

    def other_core_y(d):
        greet(dev(x, add(y, d, N), z, 1 - k))
        greet(dev(x, y, add(z, d, N), 1 - k))

    loop(1, N, other_core_y)
    pl.semaphore_wait(barrier, N * TOK - 1 + N + 2 * (N - 1))

    OM, GLS, GRS, XS, PX, BX, WG, PW, RBX, PX2, R3 = range(11)

    swap_l = x == y
    swap_r = x == z

    def om_left():
        return remote(om.at[pl.ds(0, half), :], wl, ssem.at[0], rsem.at[0], dev(y, x, z, k))

    def om_right():
        return remote(om.at[pl.ds(half, half), :], wr, ssem.at[1], rsem.at[1], dev(z, y, x, k))

    @pl.when(swap_l)
    def _():
        pltpu.make_async_copy(om.at[pl.ds(0, half), :], wl, rsem.at[0]).start()

    @pl.when(jnp.logical_not(swap_l))
    def _():
        om_left().start()

    @pl.when(swap_r)
    def _():
        pltpu.make_async_copy(om.at[pl.ds(half, half), :], wr, rsem.at[1]).start()

    @pl.when(jnp.logical_not(swap_r))
    def _():
        om_right().start()

    el, er = y * 2 + k, z * 2 + k

    def rows_of(e):
        return pl.ds(pl.multiple_of(e * CAP, CAP), CAP)

    def send_g(d):
        e = add(el, d, EXP)
        remote(
            gs.at[rows_of(e), pl.ds(0, half)], gl.at[rows_of(el), :], ssem.at[2], rsem.at[2],
            dev(x, lax.div(e, 2), z, lax.rem(e, 2)),
        ).start()
        e = add(er, d, EXP)
        remote(
            gs.at[rows_of(e), pl.ds(half, half)], gr.at[rows_of(er), :], ssem.at[3], rsem.at[3],
            dev(x, y, lax.div(e, 2), lax.rem(e, 2)),
        ).start()

    loop(1, EXP, send_g)
    pltpu.make_async_copy(
        gs.at[rows_of(el), pl.ds(0, half)], gl.at[rows_of(el), :], rsem.at[2]
    ).start()
    pltpu.make_async_copy(
        gs.at[rows_of(er), pl.ds(half, half)], gr.at[rows_of(er), :], rsem.at[3]
    ).start()

    def send_x(d):
        e = add(ex, d, EXP)
        remote(
            xs.at[rows_of(e), :], xr.at[rows_of(ex), :], ssem.at[4], rsem.at[4], (tok, e)
        ).start()

    loop(1, EXP, send_x)
    pltpu.make_async_copy(xs.at[rows_of(ex), :], xr.at[rows_of(ex), :], rsem.at[4]).start()

    def piece(i):
        return pl.ds(pl.multiple_of(i * PIECE, PIECE), PIECE)

    def to_x(left, right, dl, dr, phase):
        nls[phase] = left.astype(BF16)
        nrs[phase] = right.astype(BF16)
        sl, sr = ssem.at[5 + 2 * phase], ssem.at[6 + 2 * phase]
        rl_, rr_ = rsem.at[5 + 2 * phase], rsem.at[6 + 2 * phase]

        def go_l(d):
            b = add(y, d, N)
            remote(nls.at[phase, piece(b), :], dl.at[piece(x), :], sl, rl_, dev(y, b, z, k)).start()

        def go_r(d):
            c = add(z, d, N)
            remote(nrs.at[phase, piece(c), :], dr.at[piece(x), :], sr, rr_, dev(z, y, c, k)).start()

        loop(1, N, go_l)
        loop(1, N, go_r)
        own_l = selfsem.at[2 * phase]
        own_r = selfsem.at[2 * phase + 1]

        @pl.when(swap_l)
        def _():
            pltpu.make_async_copy(nls.at[phase, piece(y), :], dl.at[piece(x), :], rl_).start()

        @pl.when(jnp.logical_not(swap_l))
        def _():
            remote(
                nls.at[phase, piece(y), :], dl.at[piece(x), :], own_l, rl_, dev(y, y, z, k)
            ).start()

        @pl.when(swap_r)
        def _():
            pltpu.make_async_copy(nrs.at[phase, piece(z), :], dr.at[piece(x), :], rr_).start()

        @pl.when(jnp.logical_not(swap_r))
        def _():
            remote(
                nrs.at[phase, piece(z), :], dr.at[piece(x), :], own_r, rr_, dev(z, y, z, k)
            ).start()

        bytes_wait(dl, rl_)
        bytes_wait(dr, rr_)
        total = dl[...].astype(F32) + dr[...].astype(F32)
        three = nls.at[phase, pl.ds(0, 3 * PIECE), :]
        bytes_wait(three, sl)
        bytes_wait(nrs.at[phase, pl.ds(0, 3 * PIECE), :], sr)

        @pl.when(jnp.logical_not(swap_l))
        def _():
            bytes_wait(nls.at[phase, pl.ds(0, PIECE), :], own_l)

        @pl.when(jnp.logical_not(swap_r))
        def _():
            bytes_wait(nrs.at[phase, pl.ds(0, PIECE), :], own_r)

        return total

    def gram_all(s, phase):
        gm[phase] = dot_t(s, s, HIGH).astype(BF16)
        pltpu.make_async_copy(gm.at[phase], gb.at[phase, tok], gsem.at[2 * phase]).start()

        def go(d):
            t = add(tok, d, TOK)
            remote(
                gm.at[phase], gb.at[phase, tok], gsem.at[2 * phase + 1], gsem.at[2 * phase], (t, ex)
            ).start()

        loop(1, TOK, go)
        bytes_wait(gb.at[phase], gsem.at[2 * phase])
        c = lax.fori_loop(
            0, TOK, lambda i, c: c + gb[phase, i].astype(F32), jnp.zeros((RANK, RANK), F32)
        )
        bytes_wait(gb.at[phase, pl.ds(0, TOK - 1)], gsem.at[2 * phase + 1])
        return inverse_factor(c, cm, mm)

    def reduce_x(p, dst, s, r):
        pt = p.T.astype(BF16)

        def chunk(d):
            t = add(tok, d, TOK)
            cols = pl.ds(pl.multiple_of(t * wc, 128), wc)
            sp[t] = dot(pt, xr[:, cols]).astype(BF16)

            @pl.when(d < TOK)
            def _():
                remote(sp.at[t], dst.at[tok], s, r, (t, ex)).start()

        loop(1, TOK + 1, chunk)
        pltpu.make_async_copy(sp.at[tok], dst.at[tok], r).start()
        bytes_wait(dst, r)
        total = lax.fori_loop(
            0, TOK, lambda i, c: c + dst[i].astype(F32), jnp.zeros((RANK, wc), F32)
        )
        bytes_wait(sp.at[pl.ds(0, TOK - 1)], s)
        return total

    kc = 1024

    def g_dot(w_l, w_r):
        def step(j, acc):
            cols = pl.ds(pl.multiple_of(j * kc, kc), kc)
            a, b = acc
            return (
                a + dot(gl[:, cols], w_l[cols, :]),
                b + dot(gr[:, cols], w_r[cols, :]),
            )

        zero = jnp.zeros((ROWS, RANK), F32)
        return lax.fori_loop(0, half // kc, step, (zero, zero))

    bytes_wait(wl, rsem.at[0])
    bytes_wait(wr, rsem.at[1])
    bytes_wait(gl, rsem.at[2])
    bytes_wait(gr, rsem.at[3])
    left, right = g_dot(wl, wr)
    proj = to_x(left, right, pxl, pxr, 0).astype(BF16).astype(F32)
    bytes_wait(xr, rsem.at[4])

    s = reduce_x(proj, rb, ssem.at[9], rsem.at[9])
    inv = gram_all(s, 0)
    bt[tok] = jnp.dot(inv, s, precision=HIGH, preferred_element_type=F32).astype(BF16)

    def send_b(d):
        remote(
            bt.at[tok], bt.at[tok], ssem.at[10], rsem.at[10], (add(tok, d, TOK), ex)
        ).start()

    loop(1, TOK, send_b)
    bytes_wait(bt.at[pl.ds(0, TOK - 1)], rsem.at[10])

    def w_step(t, acc):
        cols = pl.ds(pl.multiple_of(t * wc, 128), wc)
        return acc + dot_t(xr[:, cols], bt[t])

    weights = lax.fori_loop(0, TOK, w_step, jnp.zeros((ROWS, RANK), F32))
    ws[...] = weights.astype(BF16)

    def go_w(d):
        a = add(x, d, N)
        remote(
            ws.at[piece(a), :], wgl.at[piece(y), :], ssem.at[11], rsem.at[11], dev(a, x, z, k)
        ).start()
        remote(
            ws.at[piece(a), :], wgr.at[piece(z), :], ssem.at[12], rsem.at[12], dev(a, y, x, k)
        ).start()

    loop(1, N, go_w)

    @pl.when(swap_l)
    def _():
        pltpu.make_async_copy(ws.at[piece(x), :], wgl.at[piece(y), :], rsem.at[11]).start()

    @pl.when(jnp.logical_not(swap_l))
    def _():
        remote(
            ws.at[piece(x), :], wgl.at[piece(y), :], selfsem.at[4], rsem.at[11], dev(x, x, z, k)
        ).start()

    @pl.when(swap_r)
    def _():
        pltpu.make_async_copy(ws.at[piece(x), :], wgr.at[piece(z), :], rsem.at[12]).start()

    @pl.when(jnp.logical_not(swap_r))
    def _():
        remote(
            ws.at[piece(x), :], wgr.at[piece(z), :], selfsem.at[5], rsem.at[12], dev(x, y, x, k)
        ).start()

    bytes_wait(wgl, rsem.at[11])
    bytes_wait(wgr, rsem.at[12])

    wlt = wgl[...].astype(F32).T.astype(BF16)
    wrt = wgr[...].astype(F32).T.astype(BF16)
    slot_l = x * N + z
    slot_r = x * N + y

    def power_chunk(d):
        t = add(tok, d, TOK)
        cols = pl.ds(pl.multiple_of(t * hc, 128), hc)
        pwl[t] = dot(wlt, gl[:, cols]).astype(BF16)
        pwr[t] = dot(wrt, gr[:, cols]).astype(BF16)

        @pl.when(d < TOK)
        def _():
            remote(
                pwl.at[t], rl.at[slot_l], ssem.at[13], rsem.at[13], (t, y * 2 + k)
            ).start()
            remote(
                pwr.at[t], rr.at[slot_r], ssem.at[14], rsem.at[14], (t, z * 2 + k)
            ).start()

    loop(1, TOK + 1, power_chunk)

    @pl.when(swap_l)
    def _():
        pltpu.make_async_copy(pwl.at[tok], rl.at[slot_l], rsem.at[13]).start()

    @pl.when(jnp.logical_not(swap_l))
    def _():
        remote(
            pwl.at[tok], rl.at[slot_l], selfsem.at[6], rsem.at[13], (tok, y * 2 + k)
        ).start()

    @pl.when(swap_r)
    def _():
        pltpu.make_async_copy(pwr.at[tok], rr.at[slot_r], rsem.at[14]).start()

    @pl.when(jnp.logical_not(swap_r))
    def _():
        remote(
            pwr.at[tok], rr.at[slot_r], selfsem.at[7], rsem.at[14], (tok, z * 2 + k)
        ).start()

    bytes_wait(rl, rsem.at[13])
    bytes_wait(rr, rsem.at[14])
    zero = jnp.zeros((RANK, hc), F32)
    sl = lax.fori_loop(0, TOK, lambda i, c: c + rl[i].astype(F32), zero)
    sr = lax.fori_loop(0, TOK, lambda i, c: c + rr[i].astype(F32), zero)
    s2 = jnp.concatenate([sl, sr], axis=1)
    inv = gram_all(s2, 1)
    right_basis = jnp.dot(inv, s2, precision=HIGH, preferred_element_type=F32).astype(BF16)

    bytes_wait(pwl.at[pl.ds(0, TOK - 1)], ssem.at[13])
    bytes_wait(pwr.at[pl.ds(0, TOK - 1)], ssem.at[14])

    @pl.when(jnp.logical_not(swap_l))
    def _():
        bytes_wait(pwl.at[0], selfsem.at[6])
        bytes_wait(ws.at[piece(0), :], selfsem.at[4])

    @pl.when(jnp.logical_not(swap_r))
    def _():
        bytes_wait(pwr.at[0], selfsem.at[7])
        bytes_wait(ws.at[piece(0), :], selfsem.at[5])

    pwl[0] = right_basis[:, :hc]
    pwr[0] = right_basis[:, hc:]

    def send_r(d):
        a = add(x, lax.div(d, N), N)
        c = add(z, lax.rem(d, N), N)
        remote(
            pwl.at[0], rbl.at[tok], ssem.at[15], rsem.at[15], dev(a, x, c, k)
        ).start()
        b = add(y, lax.rem(d, N), N)
        remote(
            pwr.at[0], rbr.at[tok], ssem.at[16], rsem.at[16], dev(a, b, x, k)
        ).start()

    loop(1, TOK, send_r)

    @pl.when(swap_l)
    def _():
        pltpu.make_async_copy(pwl.at[0], rbl.at[tok], rsem.at[15]).start()

    @pl.when(jnp.logical_not(swap_l))
    def _():
        remote(pwl.at[0], rbl.at[tok], selfsem.at[8], rsem.at[15], dev(x, x, z, k)).start()

    @pl.when(swap_r)
    def _():
        pltpu.make_async_copy(pwr.at[0], rbr.at[tok], rsem.at[16]).start()

    @pl.when(jnp.logical_not(swap_r))
    def _():
        remote(pwr.at[0], rbr.at[tok], selfsem.at[9], rsem.at[16], dev(x, y, x, k)).start()

    bytes_wait(rbl, rsem.at[15])
    bytes_wait(rbr, rsem.at[16])

    def s_step(t, acc):
        cols = pl.ds(pl.multiple_of(t * hc, 128), hc)
        a, b = acc
        return a + dot_t(gl[:, cols], rbl[t]), b + dot_t(gr[:, cols], rbr[t])

    zero = jnp.zeros((ROWS, RANK), F32)
    left, right = lax.fori_loop(0, TOK, s_step, (zero, zero))
    second = to_x(left, right, pxl2, pxr2, 1).astype(BF16).astype(F32)

    s3 = reduce_x(second, rb3, ssem.at[17], rsem.at[17])
    inv = gram_all(s3, 2)
    last = jnp.dot(inv, s3, precision=HIGH, preferred_element_type=F32)
    out[0] = last.T * scale

    @pl.when(jnp.logical_not(swap_l))
    def _():
        om_left().wait_send()
        bytes_wait(pwl.at[0], selfsem.at[8])

    @pl.when(jnp.logical_not(swap_r))
    def _():
        om_right().wait_send()
        bytes_wait(pwr.at[0], selfsem.at[9])

    part = pl.ds(0, ROWS - CAP)
    bytes_wait(gl.at[part, :], ssem.at[2])
    bytes_wait(gr.at[part, :], ssem.at[3])
    bytes_wait(xr.at[part, :], ssem.at[4])
    bytes_wait(bt.at[pl.ds(0, TOK - 1)], ssem.at[10])
    bytes_wait(ws.at[pl.ds(0, 3 * PIECE), :], ssem.at[11])
    bytes_wait(ws.at[pl.ds(0, 3 * PIECE), :], ssem.at[12])
    bytes_wait(rl.at[pl.ds(0, TOK - 1)], ssem.at[15])
    bytes_wait(rr.at[pl.ds(0, TOK - 1)], ssem.at[16])


def owners(gs, xs, om):
    hidden = gs.shape[1]
    width = xs.shape[1]
    half = hidden // 2
    wc, hc = width // TOK, half // TOK

    def vm(*shape, dtype=BF16):
        return pltpu.VMEM(shape, dtype)

    any_spec = pl.BlockSpec(memory_space=pl.ANY)
    return pl.pallas_call(
        functools.partial(body, float(width) ** 0.5),
        out_shape=jax.ShapeDtypeStruct((1, wc, RANK), F32),
        in_specs=[any_spec] * 3,
        out_specs=pl.BlockSpec(memory_space=pltpu.VMEM),
        scratch_shapes=[
            vm(ROWS, width), vm(ROWS, half), vm(ROWS, half), vm(half, RANK), vm(half, RANK),
            vm(2, ROWS, RANK), vm(2, ROWS, RANK),
            vm(ROWS, RANK), vm(ROWS, RANK), vm(ROWS, RANK), vm(ROWS, RANK),
            vm(TOK, RANK, wc), vm(TOK, RANK, wc), vm(TOK, RANK, wc), vm(TOK, RANK, wc),
            vm(ROWS, RANK), vm(ROWS, RANK), vm(ROWS, RANK),
            vm(TOK, RANK, hc), vm(TOK, RANK, hc), vm(TOK, RANK, hc), vm(TOK, RANK, hc),
            vm(TOK, RANK, hc), vm(TOK, RANK, hc),
            vm(3, RANK, RANK), vm(3, TOK, RANK, RANK),
            vm(RANK, RANK, dtype=F32), vm(RANK, RANK, dtype=F32),
            pltpu.SemaphoreType.DMA((18,)),
            pltpu.SemaphoreType.DMA((18,)),
            pltpu.SemaphoreType.DMA((6,)),
            pltpu.SemaphoreType.DMA((10,)),
        ],
        compiler_params=pltpu.CompilerParams(
            collective_id=0, has_side_effects=True, vmem_limit_bytes=58 * 1024 * 1024
        ),
        name="owners",
    )(gs, xs, om)


def shards(activations, expert_ids, out_grads, sketch_matrix):
    gs, xs = sort_rows(expert_ids, out_grads, activations)
    om = sketch_matrix.reshape(sketch_matrix.shape[1:])
    return owners(gs, xs, om)


def solution(mesh):
    return jax.shard_map(
        shards,
        mesh=mesh,
        in_specs=(
            P(("tok", "exp"), None),
            P(("tok", "exp"), None),
            P(("tok", "exp"), None, None),
            P("exp", None, None),
        ),
        out_specs=P("exp", "tok", None),
        check_vma=False,
    )
```

time: 902 us -> 820 us (0.909)
  Pallas kernels: 0 us -> 811 us
  blocking collectives: 352 us -> 0 us
  waiting for transfers between devices: 321 us -> 0 us
  other arithmetic: 83.8 us -> 0 us
  local copies, waits for them, and re-layouts: 55.5 us -> 6.59 us
  matrix products: 39.4 us -> 0 us
  starting transfers between devices: 27.6 us -> 0 us
  between operations: 14.1 us -> 0.03 us
    pallas_call x0 -> x2, Pallas kernels: none -> 811 us  [the longest x1 784 us: owners(): pl.pallas_call(functools.partial(body, float(width) ** 0.5), out_shape=ja...]
    psum x4 -> x0, blocking collectives: 352 us -> none  [the longest x3 218 us: orthonormal(): gram = lax.psum(gram.astype(jnp.bfloat16), 'tok').astype(jnp.float32)]
    psum x2 -> x0, waiting for transfers between devices: 171 us -> none  [the longest x1 85.7 us: shards(): weights = lax.psum(weight_part.astype(jnp.bfloat16), 'tok')]
    all_to_all x2 -> x0, waiting for transfers between devices: 150 us -> none  [the longest x1 150 us: shards(): lax.all_to_all(send_g, ('tok', 'exp'), split_axis=0, concat_axis=0, tiled...]
    another operation x17 -> x0, other arithmetic: 69.2 us -> none  [the longest x9 37.2 us: orthonormal(): lower = jnp.linalg.cholesky(gram)]
    dot_general x9 -> x0, matrix products: 38 us -> none  [the longest x1 9.21 us: shards(): jnp.einsum('emf,efr->emr', cols_g, right_rows, preferred_element_type=jnp...]
    gather x4 -> x0, local copies, waits for them, and re-layouts: 36.6 us -> none  [the longest x2 29.2 us: shards(): send_g = jnp.where(filled[None], grad_split[:, pair_index], 0)]
    all_to_all x2 -> x0, starting transfers between devices: 27.4 us -> none  [the longest x1 15.8 us: shards(): lax.all_to_all(send_x, ('tok', 'exp'), split_axis=0, concat_axis=0, tiled...]
  transfers between devices with their start and end apart: 4 -> 0, of which waited for: 3 -> 0; matrix products, arithmetic and copies ran while one was open for 2% -> 0% of each run, Pallas kernels for 0% -> 0%
where the time goes in v1:
time: 820 us; the launch traced here: 817 us
  Pallas kernels  811 us (99%)
    pallas_call x1, Pallas kernels, owners(): pl.pallas_call(functools.partial(body, float(width) ** 0.5), out_shape=ja...  784 us
    pallas_call x1, Pallas kernels, sort_rows(): pl.pallas_call(sort_kernel, grid=(steps,), out_shape=(jax.ShapeDtypeStruc...  27 us

profile of v1, /device:TPU:0, one launch (start us, length us, event | category | flops | bytes accessed | tf_op | source)
XLA Modules:
  0.0 817.5 jit_solution(14746575274430010764)
XLA Ops:
  0.0 0.8 copy.5.col_ids
  0.8 0.0 copy-start.1
  0.8 1.4 copy-done.1
  2.2 0.0 copy-start.2
  2.2 0.7 copy-done.2
  2.9 27.0 %sort.1 = (bf16[384,16384]{1,0:T(8,128)(2,1)}, bf16[384,6144]{1,0:T(8,128)(2,1)S(1)}) custom-call(s32[1,256]{1,0:T(1,128)S(1)} %bitcast.7, s32[256,1]{1,0:T(8,128)S(1)} %copy.5.col_ids, bf16[128,2,16384]{2,1,0:T(2,128)(2,1)} %g_ref.1, bf16[128,6144]{1,0:T(8,128)(2,1)S(1)} %copy-done.1), custom_call_target="tpu_custom_call" | custom-call | tf_op jit(solution)/shard_map/sort/pallas_call | solution.py:64
  30.0 0.0 copy-start
  30.0 2.1 copy-done
  32.0 783.8 %owners.1 = f32[1,384,128]{2,1,0:T(8,128)} custom-call(bf16[384,16384]{1,0:T(8,128)(2,1)} %get-tuple-element.7.gs, bf16[384,6144]{1,0:T(8,128)(2,1)} %copy-done, bf16[16384,128]{1,0:T(8,128)(2,1)} %bitcast.8), custom_call_target="tpu_custom_call" | custom-call | tf_op jit(solution)/shard_map/owners/pallas_call | solution.py:564
  815.9 1.6 copy.7
Async XLA Ops:
  0.8 1.4 copy-start.1
  2.2 0.7 copy-start.2
  30.0 2.1 copy-start

commit v2 on v1

--- a/solution.py
+++ b/solution.py
@@ -185,14 +185,25 @@
 
     OM, GLS, GRS, XS, PX, BX, WG, PW, RBX, PX2, R3 = range(11)
 
-    swap_l = x == y
-    swap_r = x == z
+    shift_l = lax.rem(y - z + N, N)
+    shift_r = lax.rem(y - z + N + 2, N)
+    swap_l = shift_l == 0
+    swap_r = shift_r == 0
+    xl = add(x, shift_l, N)
+    xd = add(x, shift_r, N)
+
+    def left_y(at_x, to_x, c):
+        return lax.rem(to_x - at_x + c + N, N)
+
+    def right_z(at_x, to_x, b):
+        return lax.rem(at_x + b + 2 - to_x + N, N)
+
 
     def om_left():
-        return remote(om.at[pl.ds(0, half), :], wl, ssem.at[0], rsem.at[0], dev(y, x, z, k))
+        return remote(om.at[pl.ds(0, half), :], wl, ssem.at[0], rsem.at[0], dev(add(x, N - shift_l, N), y, z, k))
 
     def om_right():
-        return remote(om.at[pl.ds(half, half), :], wr, ssem.at[1], rsem.at[1], dev(z, y, x, k))
+        return remote(om.at[pl.ds(half, half), :], wr, ssem.at[1], rsem.at[1], dev(add(x, N - shift_r, N), y, z, k))
 
     @pl.when(swap_l)
     def _():
@@ -211,28 +222,29 @@
         om_right().start()
 
     el, er = y * 2 + k, z * 2 + k
+    own_el, own_er = xl * 2 + k, xd * 2 + k
 
     def rows_of(e):
         return pl.ds(pl.multiple_of(e * CAP, CAP), CAP)
 
     def send_g(d):
-        e = add(el, d, EXP)
+        e = add(own_el, d, EXP)
         remote(
             gs.at[rows_of(e), pl.ds(0, half)], gl.at[rows_of(el), :], ssem.at[2], rsem.at[2],
-            dev(x, lax.div(e, 2), z, lax.rem(e, 2)),
-        ).start()
-        e = add(er, d, EXP)
+            dev(x, left_y(x, lax.div(e, 2), z), z, lax.rem(e, 2)),
+        ).start()
+        e = add(own_er, d, EXP)
         remote(
             gs.at[rows_of(e), pl.ds(half, half)], gr.at[rows_of(er), :], ssem.at[3], rsem.at[3],
-            dev(x, y, lax.div(e, 2), lax.rem(e, 2)),
+            dev(x, y, right_z(x, lax.div(e, 2), y), lax.rem(e, 2)),
         ).start()
 
     loop(1, EXP, send_g)
     pltpu.make_async_copy(
-        gs.at[rows_of(el), pl.ds(0, half)], gl.at[rows_of(el), :], rsem.at[2]
+        gs.at[rows_of(own_el), pl.ds(0, half)], gl.at[rows_of(el), :], rsem.at[2]
     ).start()
     pltpu.make_async_copy(
-        gs.at[rows_of(er), pl.ds(half, half)], gr.at[rows_of(er), :], rsem.at[3]
+        gs.at[rows_of(own_er), pl.ds(half, half)], gr.at[rows_of(er), :], rsem.at[3]
     ).start()
 
     def send_x(d):
@@ -255,11 +267,11 @@
 
         def go_l(d):
             b = add(y, d, N)
-            remote(nls.at[phase, piece(b), :], dl.at[piece(x), :], sl, rl_, dev(y, b, z, k)).start()
+            remote(nls.at[phase, piece(b), :], dl.at[piece(x), :], sl, rl_, dev(xl, b, z, k)).start()
 
         def go_r(d):
             c = add(z, d, N)
-            remote(nrs.at[phase, piece(c), :], dr.at[piece(x), :], sr, rr_, dev(z, y, c, k)).start()
+            remote(nrs.at[phase, piece(c), :], dr.at[piece(x), :], sr, rr_, dev(xd, y, c, k)).start()
 
         loop(1, N, go_l)
         loop(1, N, go_r)
@@ -273,7 +285,7 @@
         @pl.when(jnp.logical_not(swap_l))
         def _():
             remote(
-                nls.at[phase, piece(y), :], dl.at[piece(x), :], own_l, rl_, dev(y, y, z, k)
+                nls.at[phase, piece(y), :], dl.at[piece(x), :], own_l, rl_, dev(xl, y, z, k)
             ).start()
 
         @pl.when(swap_r)
@@ -283,7 +295,7 @@
         @pl.when(jnp.logical_not(swap_r))
         def _():
             remote(
-                nrs.at[phase, piece(z), :], dr.at[piece(x), :], own_r, rr_, dev(z, y, z, k)
+                nrs.at[phase, piece(z), :], dr.at[piece(x), :], own_r, rr_, dev(xd, y, z, k)
             ).start()
 
         bytes_wait(dl, rl_)
@@ -386,10 +398,12 @@
     def go_w(d):
         a = add(x, d, N)
         remote(
-            ws.at[piece(a), :], wgl.at[piece(y), :], ssem.at[11], rsem.at[11], dev(a, x, z, k)
-        ).start()
-        remote(
-            ws.at[piece(a), :], wgr.at[piece(z), :], ssem.at[12], rsem.at[12], dev(a, y, x, k)
+            ws.at[piece(a), :], wgl.at[piece(y), :], ssem.at[11], rsem.at[11],
+            dev(a, left_y(a, x, z), z, k),
+        ).start()
+        remote(
+            ws.at[piece(a), :], wgr.at[piece(z), :], ssem.at[12], rsem.at[12],
+            dev(a, y, right_z(a, x, y), k),
         ).start()
 
     loop(1, N, go_w)
@@ -401,7 +415,8 @@
     @pl.when(jnp.logical_not(swap_l))
     def _():
         remote(
-            ws.at[piece(x), :], wgl.at[piece(y), :], selfsem.at[4], rsem.at[11], dev(x, x, z, k)
+            ws.at[piece(x), :], wgl.at[piece(y), :], selfsem.at[4], rsem.at[11],
+            dev(x, left_y(x, x, z), z, k),
         ).start()
 
     @pl.when(swap_r)
@@ -411,7 +426,8 @@
     @pl.when(jnp.logical_not(swap_r))
     def _():
         remote(
-            ws.at[piece(x), :], wgr.at[piece(z), :], selfsem.at[5], rsem.at[12], dev(x, y, x, k)
+            ws.at[piece(x), :], wgr.at[piece(z), :], selfsem.at[5], rsem.at[12],
+            dev(x, y, right_z(x, x, y), k),
         ).start()
 
     bytes_wait(wgl, rsem.at[11])
@@ -431,10 +447,10 @@
         @pl.when(d < TOK)
         def _():
             remote(
-                pwl.at[t], rl.at[slot_l], ssem.at[13], rsem.at[13], (t, y * 2 + k)
+                pwl.at[t], rl.at[slot_l], ssem.at[13], rsem.at[13], (t, own_el)
             ).start()
             remote(
-                pwr.at[t], rr.at[slot_r], ssem.at[14], rsem.at[14], (t, z * 2 + k)
+                pwr.at[t], rr.at[slot_r], ssem.at[14], rsem.at[14], (t, own_er)
             ).start()
 
     loop(1, TOK + 1, power_chunk)
@@ -446,7 +462,7 @@
     @pl.when(jnp.logical_not(swap_l))
     def _():
         remote(
-            pwl.at[tok], rl.at[slot_l], selfsem.at[6], rsem.at[13], (tok, y * 2 + k)
+            pwl.at[tok], rl.at[slot_l], selfsem.at[6], rsem.at[13], (tok, own_el)
         ).start()
 
     @pl.when(swap_r)
@@ -456,7 +472,7 @@
     @pl.when(jnp.logical_not(swap_r))
     def _():
         remote(
-            pwr.at[tok], rr.at[slot_r], selfsem.at[7], rsem.at[14], (tok, z * 2 + k)
+            pwr.at[tok], rr.at[slot_r], selfsem.at[7], rsem.at[14], (tok, own_er)
         ).start()
 
     bytes_wait(rl, rsem.at[13])
@@ -488,11 +504,13 @@
         a = add(x, lax.div(d, N), N)
         c = add(z, lax.rem(d, N), N)
         remote(
-            pwl.at[0], rbl.at[tok], ssem.at[15], rsem.at[15], dev(a, x, c, k)
+            pwl.at[0], rbl.at[tok], ssem.at[15], rsem.at[15],
+            dev(a, left_y(a, x, c), c, k),
         ).start()
         b = add(y, lax.rem(d, N), N)
         remote(
-            pwr.at[0], rbr.at[tok], ssem.at[16], rsem.at[16], dev(a, b, x, k)
+            pwr.at[0], rbr.at[tok], ssem.at[16], rsem.at[16],
+            dev(a, b, right_z(a, x, b), k),
         ).start()
 
     loop(1, TOK, send_r)
@@ -503,7 +521,7 @@
 
     @pl.when(jnp.logical_not(swap_l))
     def _():
-        remote(pwl.at[0], rbl.at[tok], selfsem.at[8], rsem.at[15], dev(x, x, z, k)).start()
+        remote(pwl.at[0], rbl.at[tok], selfsem.at[8], rsem.at[15], dev(x, left_y(x, x, z), z, k)).start()
 
     @pl.when(swap_r)
     def _():
@@ -511,7 +529,7 @@
 
     @pl.when(jnp.logical_not(swap_r))
     def _():
-        remote(pwr.at[0], rbr.at[tok], selfsem.at[9], rsem.at[16], dev(x, y, x, k)).start()
+        remote(pwr.at[0], rbr.at[tok], selfsem.at[9], rsem.at[16], dev(x, y, right_z(x, x, y), k)).start()
 
     bytes_wait(rbl, rsem.at[15])
     bytes_wait(rbr, rsem.at[16])

time: 820 us -> 481 us (0.59)
  Pallas kernels: 811 us -> 474 us
    pallas_call x1, Pallas kernels: 784 us -> 447 us  [owners(): pl.pallas_call(functools.partial(body, float(width) ** 0.5), out_shape=ja...]
where the time goes in v2:
time: 481 us; the launch traced here: 480 us
  Pallas kernels  474 us (99%)
  local copies, waits for them, and re-layouts  6.59 us (1%)
    pallas_call x1, Pallas kernels, owners(): pl.pallas_call(functools.partial(body, float(width) ** 0.5), out_shape=ja...  447 us
    pallas_call x1, Pallas kernels, sort_rows(): pl.pallas_call(sort_kernel, grid=(steps,), out_shape=(jax.ShapeDtypeStruc...  27 us

profile of v2, /device:TPU:0, one launch (start us, length us, event | category | flops | bytes accessed | tf_op | source)
XLA Modules:
  0.0 480.3 jit_solution(975600399365535488)
XLA Ops:
  0.0 0.8 copy.5.col_ids
  0.8 0.0 copy-start.1
  0.8 1.4 copy-done.1
  2.2 0.0 copy-start.2
  2.2 0.7 copy-done.2
  2.9 27.0 %sort.1 = (bf16[384,16384]{1,0:T(8,128)(2,1)}, bf16[384,6144]{1,0:T(8,128)(2,1)S(1)}) custom-call(s32[1,256]{1,0:T(1,128)S(1)} %bitcast.7, s32[256,1]{1,0:T(8,128)S(1)} %copy.5.col_ids, bf16[128,2,16384]{2,1,0:T(2,128)(2,1)} %g_ref.1, bf16[128,6144]{1,0:T(8,128)(2,1)S(1)} %copy-done.1), custom_call_target="tpu_custom_call" | custom-call | tf_op jit(solution)/shard_map/sort/pallas_call | solution.py:64
  30.0 0.0 copy-start
  30.0 2.1 copy-done
  32.0 446.7 %owners.1 = f32[1,384,128]{2,1,0:T(8,128)} custom-call(bf16[384,16384]{1,0:T(8,128)(2,1)} %get-tuple-element.7.gs, bf16[384,6144]{1,0:T(8,128)(2,1)} %copy-done, bf16[16384,128]{1,0:T(8,128)(2,1)} %bitcast.8), custom_call_target="tpu_custom_call" | custom-call | tf_op jit(solution)/shard_map/owners/pallas_call | solution.py:582
  478.7 1.6 copy.7
Async XLA Ops:
  0.8 1.4 copy-start.1
  2.2 0.7 copy-start.2
  30.0 2.1 copy-start

commit v3 on v2

--- a/solution.py
+++ b/solution.py
@@ -32,9 +32,9 @@
     )
 
 
-def sort_kernel(row_ids, col_ids, g_ref, x_ref, gs_ref, xs_ref, pick):
+def sort_kernel(row_ids, col_ids, g_ref, x_ref, gs_ref, xs_ref, pick, pick_x):
     pairs = row_ids.shape[1]
-    toks = x_ref.shape[0]
+    toks, top, hc = g_ref.shape
 
     @pl.when(pl.program_id(0) == 0)
     def _():
@@ -47,19 +47,22 @@
         slot = ids * CAP + rank
         hot = lax.broadcasted_iota(jnp.int32, (ROWS, pairs), 0) == slot
         pick[...] = hot.astype(F32).astype(BF16)
-
-    first = pick[:, :toks]
-    second = pick[:, toks:]
-    gs = dot(first, g_ref[:, 0, :]) + dot(second, g_ref[:, 1, :])
-    gs_ref[...] = gs.astype(BF16)
-    xs_ref[...] = dot(first + second, x_ref[...]).astype(BF16)
-
-
-def sort_rows(expert_ids, out_grads, activations, steps=16):
+        token = lax.broadcasted_iota(jnp.int32, (pairs, toks), 0) - top * lax.broadcasted_iota(
+            jnp.int32, (pairs, toks), 1
+        )
+        of_token = ((token >= 0) & (token < top)).astype(F32).astype(BF16)
+        pick_x[...] = dot(pick[...], of_token).astype(BF16)
+
+    gs_ref[...] = dot(pick[...], g_ref[...].reshape(pairs, hc)).astype(BF16)
+    xs_ref[...] = dot(pick_x[...], x_ref[...]).astype(BF16)
+
+
+def sort_rows(expert_ids, out_grads, activations, steps=8):
     toks, top = expert_ids.shape
+    pairs = toks * top
     hidden = out_grads.shape[2]
     width = activations.shape[1]
-    ids = expert_ids.T.reshape(1, toks * top)
+    ids = expert_ids.reshape(1, pairs)
     hc, wc = hidden // steps, width // steps
     return pl.pallas_call(
         sort_kernel,
@@ -69,8 +72,8 @@
             jax.ShapeDtypeStruct((ROWS, width), BF16),
         ),
         in_specs=[
-            pl.BlockSpec((1, toks * top), lambda i: (0, 0)),
-            pl.BlockSpec((toks * top, 1), lambda i: (0, 0)),
+            pl.BlockSpec((1, pairs), lambda i: (0, 0)),
+            pl.BlockSpec((pairs, 1), lambda i: (0, 0)),
             pl.BlockSpec((toks, top, hc), lambda i: (0, 0, i)),
             pl.BlockSpec((toks, wc), lambda i: (0, i)),
         ],
@@ -78,10 +81,10 @@
             pl.BlockSpec((ROWS, hc), lambda i: (0, i)),
             pl.BlockSpec((ROWS, wc), lambda i: (0, i)),
         ),
-        scratch_shapes=[pltpu.VMEM((ROWS, toks * top), BF16)],
+        scratch_shapes=[pltpu.VMEM((ROWS, pairs), BF16), pltpu.VMEM((ROWS, toks), BF16)],
         compiler_params=pltpu.CompilerParams(vmem_limit_bytes=40 * 1024 * 1024),
         name="sort",
-    )(ids, ids.reshape(toks * top, 1), out_grads, activations)
+    )(ids, ids.reshape(pairs, 1), out_grads, activations)
 
 
 def bytes_wait(ref, sem):
@@ -95,21 +98,21 @@
     mm[...] = (rows == cols).astype(F32)
     prow = lax.broadcasted_iota(jnp.int32, (PANEL, RANK), 0)
     pcol = lax.broadcasted_iota(jnp.int32, (PANEL, RANK), 1)
-    srow = lax.broadcasted_iota(jnp.int32, (PANEL, 1), 0)
 
     def panel(p, carry):
         base = pl.multiple_of(p * PANEL, PANEL)
-        a = pltpu.roll(cm[pl.ds(base, PANEL), :], lax.rem(RANK - base, RANK), 1)
+        a = cm[pl.ds(base, PANEL), :]
         m = mm[pl.ds(base, PANEL), :]
+        near = pltpu.roll(a, lax.rem(RANK - base, RANK), 1)
+        block = [jnp.broadcast_to(near[:, i : i + 1], (PANEL, RANK)) for i in range(PANEL)]
         for i in range(PANEL):
-            ra = a[i : i + 1, :]
-            rm = m[i : i + 1, :]
-            r = lax.rsqrt(a[i : i + 1, i : i + 1])
-            col = jnp.where(srow > i, a[:, i : i + 1] * (r * r), 0.0)
-            a = jnp.where(prow == i, a * r, a - col * ra)
-            m = jnp.where(prow == i, m * r, m - col * rm)
+            r = lax.rsqrt(block[i][i : i + 1, :])
+            mult = jnp.where(prow > i, block[i] * (r * r), 0.0)
+            for j in range(i + 1, PANEL):
+                block[j] = block[j] - mult * block[j][i : i + 1, :]
+            a = jnp.where(prow == i, a * r, a - mult * a[i : i + 1, :])
+            m = jnp.where(prow == i, m * r, m - mult * m[i : i + 1, :])
         mm[pl.ds(base, PANEL), :] = m
-        a = pltpu.roll(a, base, 1)
         left = jnp.where(pcol >= base + PANEL, a, 0.0)
         both = jnp.concatenate([a, m], axis=1)
         change = lax.dot_general(
@@ -131,7 +134,7 @@
     nls, nrs, pxl, pxr, pxl2, pxr2,
     sp, rb, rb3, bt,
     ws, wgl, wgr,
-    pwl, pwr, rl, rr, rbl, rbr,
+    pwl, pwr, rl1, rr1, mid_l, mid_r, rl2, rr2, own_rl, own_rr, rbl, rbr,
     gm, gb, cm, mm,
     ssem, rsem, gsem, selfsem,
 ):
@@ -183,31 +186,42 @@
     loop(1, N, other_core_y)
     pl.semaphore_wait(barrier, N * TOK - 1 + N + 2 * (N - 1))
 
-    OM, GLS, GRS, XS, PX, BX, WG, PW, RBX, PX2, R3 = range(11)
-
-    shift_l = lax.rem(y - z + N, N)
-    shift_r = lax.rem(y - z + N + 2, N)
-    swap_l = shift_l == 0
-    swap_r = shift_r == 0
-    xl = add(x, shift_l, N)
+    shift_r = lax.rem(N - z, N)
+    swap_l = y == 0
+    swap_r = z == 0
+    xl = add(x, y, N)
     xd = add(x, shift_r, N)
-
-    def left_y(at_x, to_x, c):
-        return lax.rem(to_x - at_x + c + N, N)
-
-    def right_z(at_x, to_x, b):
-        return lax.rem(at_x + b + 2 - to_x + N, N)
-
+    own_el, own_er = xl * 2 + k, xd * 2 + k
+
+    def left_y(at_x, to_x):
+        return lax.rem(to_x - at_x + N, N)
+
+    def right_z(at_x, to_x):
+        return lax.rem(at_x - to_x + N, N)
+
+    quarter = half // N
+
+    def om_rows(i):
+        return pl.ds(pl.multiple_of(i * quarter, quarter), quarter)
+
+    def om_right_rows(i):
+        return pl.ds(pl.multiple_of(half + i * quarter, quarter), quarter)
 
     def om_left():
-        return remote(om.at[pl.ds(0, half), :], wl, ssem.at[0], rsem.at[0], dev(add(x, N - shift_l, N), y, z, k))
+        return remote(
+            om.at[om_rows(z), :], wl.at[om_rows(z), :], ssem.at[0], rsem.at[0],
+            dev(add(x, N - y, N), y, z, k),
+        )
 
     def om_right():
-        return remote(om.at[pl.ds(half, half), :], wr, ssem.at[1], rsem.at[1], dev(add(x, N - shift_r, N), y, z, k))
+        return remote(
+            om.at[om_right_rows(y), :], wr.at[om_rows(y), :], ssem.at[1], rsem.at[1],
+            dev(add(x, z, N), y, z, k),
+        )
 
     @pl.when(swap_l)
     def _():
-        pltpu.make_async_copy(om.at[pl.ds(0, half), :], wl, rsem.at[0]).start()
+        pltpu.make_async_copy(om.at[om_rows(z), :], wl.at[om_rows(z), :], rsem.at[0]).start()
 
     @pl.when(jnp.logical_not(swap_l))
     def _():
@@ -215,14 +229,13 @@
 
     @pl.when(swap_r)
     def _():
-        pltpu.make_async_copy(om.at[pl.ds(half, half), :], wr, rsem.at[1]).start()
+        pltpu.make_async_copy(om.at[om_right_rows(y), :], wr.at[om_rows(y), :], rsem.at[1]).start()
 
     @pl.when(jnp.logical_not(swap_r))
     def _():
         om_right().start()
 
     el, er = y * 2 + k, z * 2 + k
-    own_el, own_er = xl * 2 + k, xd * 2 + k
 
     def rows_of(e):
         return pl.ds(pl.multiple_of(e * CAP, CAP), CAP)
@@ -231,12 +244,12 @@
         e = add(own_el, d, EXP)
         remote(
             gs.at[rows_of(e), pl.ds(0, half)], gl.at[rows_of(el), :], ssem.at[2], rsem.at[2],
-            dev(x, left_y(x, lax.div(e, 2), z), z, lax.rem(e, 2)),
+            dev(x, left_y(x, lax.div(e, 2)), z, lax.rem(e, 2)),
         ).start()
         e = add(own_er, d, EXP)
         remote(
             gs.at[rows_of(e), pl.ds(half, half)], gr.at[rows_of(er), :], ssem.at[3], rsem.at[3],
-            dev(x, y, right_z(x, lax.div(e, 2), y), lax.rem(e, 2)),
+            dev(x, y, right_z(x, lax.div(e, 2)), lax.rem(e, 2)),
         ).start()
 
     loop(1, EXP, send_g)
@@ -256,6 +269,21 @@
     loop(1, EXP, send_x)
     pltpu.make_async_copy(xs.at[rows_of(ex), :], xr.at[rows_of(ex), :], rsem.at[4]).start()
 
+    bytes_wait(wl.at[om_rows(z), :], rsem.at[0])
+    bytes_wait(wr.at[om_rows(y), :], rsem.at[1])
+
+    def om_share(d):
+        remote(
+            wl.at[om_rows(z), :], wl.at[om_rows(z), :], ssem.at[18], rsem.at[18],
+            dev(x, y, add(z, d, N), k),
+        ).start()
+        remote(
+            wr.at[om_rows(y), :], wr.at[om_rows(y), :], ssem.at[19], rsem.at[19],
+            dev(x, add(y, d, N), z, k),
+        ).start()
+
+    loop(1, N, om_share)
+
     def piece(i):
         return pl.ds(pl.multiple_of(i * PIECE, PIECE), PIECE)
 
@@ -275,8 +303,8 @@
 
         loop(1, N, go_l)
         loop(1, N, go_r)
-        own_l = selfsem.at[2 * phase]
-        own_r = selfsem.at[2 * phase + 1]
+        own_l = selfsem.at[12 + 2 * phase]
+        own_r = selfsem.at[13 + 2 * phase]
 
         @pl.when(swap_l)
         def _():
@@ -368,8 +396,9 @@
         zero = jnp.zeros((ROWS, RANK), F32)
         return lax.fori_loop(0, half // kc, step, (zero, zero))
 
-    bytes_wait(wl, rsem.at[0])
-    bytes_wait(wr, rsem.at[1])
+    most = pl.ds(0, 3 * quarter)
+    bytes_wait(wl.at[most, :], rsem.at[18])
+    bytes_wait(wr.at[most, :], rsem.at[19])
     bytes_wait(gl, rsem.at[2])
     bytes_wait(gr, rsem.at[3])
     left, right = g_dot(wl, wr)
@@ -399,11 +428,11 @@
         a = add(x, d, N)
         remote(
             ws.at[piece(a), :], wgl.at[piece(y), :], ssem.at[11], rsem.at[11],
-            dev(a, left_y(a, x, z), z, k),
+            dev(a, left_y(a, x), z, k),
         ).start()
         remote(
             ws.at[piece(a), :], wgr.at[piece(z), :], ssem.at[12], rsem.at[12],
-            dev(a, y, right_z(a, x, y), k),
+            dev(a, y, right_z(a, x), k),
         ).start()
 
     loop(1, N, go_w)
@@ -415,8 +444,8 @@
     @pl.when(jnp.logical_not(swap_l))
     def _():
         remote(
-            ws.at[piece(x), :], wgl.at[piece(y), :], selfsem.at[4], rsem.at[11],
-            dev(x, left_y(x, x, z), z, k),
+            ws.at[piece(x), :], wgl.at[piece(y), :], selfsem.at[16], rsem.at[11],
+            dev(x, left_y(x, x), z, k),
         ).start()
 
     @pl.when(swap_r)
@@ -426,8 +455,8 @@
     @pl.when(jnp.logical_not(swap_r))
     def _():
         remote(
-            ws.at[piece(x), :], wgr.at[piece(z), :], selfsem.at[5], rsem.at[12],
-            dev(x, y, right_z(x, x, y), k),
+            ws.at[piece(x), :], wgr.at[piece(z), :], selfsem.at[17], rsem.at[12],
+            dev(x, y, right_z(x, x), k),
         ).start()
 
     bytes_wait(wgl, rsem.at[11])
@@ -435,112 +464,149 @@
 
     wlt = wgl[...].astype(F32).T.astype(BF16)
     wrt = wgr[...].astype(F32).T.astype(BF16)
-    slot_l = x * N + z
-    slot_r = x * N + y
-
-    def power_chunk(d):
-        t = add(tok, d, TOK)
-        cols = pl.ds(pl.multiple_of(t * hc, 128), hc)
-        pwl[t] = dot(wlt, gl[:, cols]).astype(BF16)
-        pwr[t] = dot(wrt, gr[:, cols]).astype(BF16)
-
-        @pl.when(d < TOK)
+
+    def cols_of(b, c):
+        return pl.ds(pl.multiple_of((b * N + c) * hc, 128), hc)
+
+    def power_group(d):
+        g = add(z, d, N)
+
+        def left_one(b):
+            pwl[g, b] = dot(wlt, gl[:, cols_of(b, g)]).astype(BF16)
+
+        loop(0, N, left_one)
+
+        @pl.when(d < N)
+        def _():
+            remote(pwl.at[g], rl1.at[z], ssem.at[13], rsem.at[13], dev(x, y, g, k)).start()
+
+        g2 = add(y, d, N)
+
+        def right_one(c):
+            pwr[g2, c] = dot(wrt, gr[:, cols_of(g2, c)]).astype(BF16)
+
+        loop(0, N, right_one)
+
+        @pl.when(d < N)
+        def _():
+            remote(pwr.at[g2], rr1.at[y], ssem.at[14], rsem.at[14], dev(x, g2, z, k)).start()
+
+    loop(1, N + 1, power_group)
+    part3 = pl.ds(0, N - 1)
+    bytes_wait(rl1.at[part3], rsem.at[13])
+
+    def sum_along(d, own, got, me, other):
+        def term(i, acc):
+            return acc + got[add(me, i, N), other].astype(F32)
+
+        return lax.fori_loop(1, N, term, own[me, other].astype(F32))
+
+    def stage2_left(i):
+        b = add(y, i, N)
+        mid_l[b] = sum_along(i, pwl, rl1, z, b).astype(BF16)
+
+        @pl.when(jnp.logical_or(i < N, jnp.logical_not(swap_l)))
         def _():
             remote(
-                pwl.at[t], rl.at[slot_l], ssem.at[13], rsem.at[13], (t, own_el)
+                mid_l.at[b], rl2.at[x], selfsem.at[i], rsem.at[20], dev(xl, b, z, k)
             ).start()
+
+    def stage2_right(i):
+        c = add(z, i, N)
+        mid_r[c] = sum_along(i, pwr, rr1, y, c).astype(BF16)
+
+        @pl.when(jnp.logical_or(i < N, jnp.logical_not(swap_r)))
+        def _():
             remote(
-                pwr.at[t], rr.at[slot_r], ssem.at[14], rsem.at[14], (t, own_er)
+                mid_r.at[c], rr2.at[x], selfsem.at[N + 1 + i], rsem.at[21], dev(xd, y, c, k)
             ).start()
 
-    loop(1, TOK + 1, power_chunk)
+    loop(1, N + 1, stage2_left)
 
     @pl.when(swap_l)
     def _():
-        pltpu.make_async_copy(pwl.at[tok], rl.at[slot_l], rsem.at[13]).start()
-
-    @pl.when(jnp.logical_not(swap_l))
-    def _():
-        remote(
-            pwl.at[tok], rl.at[slot_l], selfsem.at[6], rsem.at[13], (tok, own_el)
-        ).start()
+        pltpu.make_async_copy(mid_l.at[y], rl2.at[x], rsem.at[20]).start()
+
+    bytes_wait(rr1.at[part3], rsem.at[14])
+    loop(1, N + 1, stage2_right)
 
     @pl.when(swap_r)
     def _():
-        pltpu.make_async_copy(pwr.at[tok], rr.at[slot_r], rsem.at[14]).start()
-
-    @pl.when(jnp.logical_not(swap_r))
-    def _():
-        remote(
-            pwr.at[tok], rr.at[slot_r], selfsem.at[7], rsem.at[14], (tok, own_er)
-        ).start()
-
-    bytes_wait(rl, rsem.at[13])
-    bytes_wait(rr, rsem.at[14])
+        pltpu.make_async_copy(mid_r.at[z], rr2.at[x], rsem.at[21]).start()
+
+    bytes_wait(rl2, rsem.at[20])
+    bytes_wait(rr2, rsem.at[21])
     zero = jnp.zeros((RANK, hc), F32)
-    sl = lax.fori_loop(0, TOK, lambda i, c: c + rl[i].astype(F32), zero)
-    sr = lax.fori_loop(0, TOK, lambda i, c: c + rr[i].astype(F32), zero)
+    sl = lax.fori_loop(0, N, lambda i, c: c + rl2[i].astype(F32), zero)
+    sr = lax.fori_loop(0, N, lambda i, c: c + rr2[i].astype(F32), zero)
     s2 = jnp.concatenate([sl, sr], axis=1)
     inv = gram_all(s2, 1)
     right_basis = jnp.dot(inv, s2, precision=HIGH, preferred_element_type=F32).astype(BF16)
 
-    bytes_wait(pwl.at[pl.ds(0, TOK - 1)], ssem.at[13])
-    bytes_wait(pwr.at[pl.ds(0, TOK - 1)], ssem.at[14])
+    own_rl[...] = right_basis[:, :hc]
+    own_rr[...] = right_basis[:, hc:]
+
+    def send_r(d):
+        a = add(x, d, N)
+        remote(
+            own_rl, rbl.at[z, y], ssem.at[15], rsem.at[15], dev(a, left_y(a, x), z, k)
+        ).start()
+        remote(
+            own_rr, rbr.at[y, z], ssem.at[16], rsem.at[16], dev(a, y, right_z(a, x), k)
+        ).start()
+
+    loop(1, N, send_r)
+
+    @pl.when(swap_l)
+    def _():
+        pltpu.make_async_copy(own_rl, rbl.at[z, y], rsem.at[15]).start()
 
     @pl.when(jnp.logical_not(swap_l))
     def _():
-        bytes_wait(pwl.at[0], selfsem.at[6])
-        bytes_wait(ws.at[piece(0), :], selfsem.at[4])
+        remote(own_rl, rbl.at[z, y], selfsem.at[10], rsem.at[15], dev(x, 0, z, k)).start()
+
+    @pl.when(swap_r)
+    def _():
+        pltpu.make_async_copy(own_rr, rbr.at[y, z], rsem.at[16]).start()
 
     @pl.when(jnp.logical_not(swap_r))
     def _():
-        bytes_wait(pwr.at[0], selfsem.at[7])
-        bytes_wait(ws.at[piece(0), :], selfsem.at[5])
-
-    pwl[0] = right_basis[:, :hc]
-    pwr[0] = right_basis[:, hc:]
-
-    def send_r(d):
-        a = add(x, lax.div(d, N), N)
-        c = add(z, lax.rem(d, N), N)
-        remote(
-            pwl.at[0], rbl.at[tok], ssem.at[15], rsem.at[15],
-            dev(a, left_y(a, x, c), c, k),
-        ).start()
-        b = add(y, lax.rem(d, N), N)
-        remote(
-            pwr.at[0], rbr.at[tok], ssem.at[16], rsem.at[16],
-            dev(a, b, right_z(a, x, b), k),
-        ).start()
-
-    loop(1, TOK, send_r)
-
-    @pl.when(swap_l)
-    def _():
-        pltpu.make_async_copy(pwl.at[0], rbl.at[tok], rsem.at[15]).start()
-
-    @pl.when(jnp.logical_not(swap_l))
-    def _():
-        remote(pwl.at[0], rbl.at[tok], selfsem.at[8], rsem.at[15], dev(x, left_y(x, x, z), z, k)).start()
-
-    @pl.when(swap_r)
-    def _():
-        pltpu.make_async_copy(pwr.at[0], rbr.at[tok], rsem.at[16]).start()
-
-    @pl.when(jnp.logical_not(swap_r))
-    def _():
-        remote(pwr.at[0], rbr.at[tok], selfsem.at[9], rsem.at[16], dev(x, y, right_z(x, x, y), k)).start()
-
-    bytes_wait(rbl, rsem.at[15])
-    bytes_wait(rbr, rsem.at[16])
-
-    def s_step(t, acc):
-        cols = pl.ds(pl.multiple_of(t * hc, 128), hc)
-        a, b = acc
-        return a + dot_t(gl[:, cols], rbl[t]), b + dot_t(gr[:, cols], rbr[t])
+        remote(own_rr, rbr.at[y, z], selfsem.at[11], rsem.at[16], dev(x, y, 0, k)).start()
+
+    bytes_wait(rbl.at[z], rsem.at[15])
+
+    def share_l(d):
+        remote(
+            rbl.at[z], rbl.at[z], ssem.at[22], rsem.at[22], dev(x, y, add(z, d, N), k)
+        ).start()
+
+    loop(1, N, share_l)
+    bytes_wait(rbr.at[y], rsem.at[16])
+
+    def share_r(d):
+        remote(
+            rbr.at[y], rbr.at[y], ssem.at[23], rsem.at[23], dev(x, add(y, d, N), z, k)
+        ).start()
+
+    loop(1, N, share_r)
+
+    def left_group(g, acc):
+        return lax.fori_loop(
+            0, N, lambda b, t: t + dot_t(gl[:, cols_of(b, g)], rbl[g, b]), acc
+        )
+
+    def right_group(g, acc):
+        return lax.fori_loop(
+            0, N, lambda c, t: t + dot_t(gr[:, cols_of(g, c)], rbr[g, c]), acc
+        )
 
     zero = jnp.zeros((ROWS, RANK), F32)
-    left, right = lax.fori_loop(0, TOK, s_step, (zero, zero))
+    left = left_group(z, zero)
+    right = right_group(y, zero)
+    bytes_wait(rbl.at[part3], rsem.at[22])
+    bytes_wait(rbr.at[part3], rsem.at[23])
+    left = lax.fori_loop(1, N, lambda d, t: left_group(add(z, d, N), t), left)
+    right = lax.fori_loop(1, N, lambda d, t: right_group(add(y, d, N), t), right)
     second = to_x(left, right, pxl2, pxr2, 1).astype(BF16).astype(F32)
 
     s3 = reduce_x(second, rb3, ssem.at[17], rsem.at[17])
@@ -551,13 +617,28 @@
     @pl.when(jnp.logical_not(swap_l))
     def _():
         om_left().wait_send()
-        bytes_wait(pwl.at[0], selfsem.at[8])
+        bytes_wait(ws.at[piece(0), :], selfsem.at[16])
+        bytes_wait(mid_l.at[0], selfsem.at[N])
+        bytes_wait(own_rl, selfsem.at[10])
 
     @pl.when(jnp.logical_not(swap_r))
     def _():
         om_right().wait_send()
-        bytes_wait(pwr.at[0], selfsem.at[9])
-
+        bytes_wait(ws.at[piece(0), :], selfsem.at[17])
+        bytes_wait(mid_r.at[0], selfsem.at[2 * N + 1])
+        bytes_wait(own_rr, selfsem.at[11])
+
+    def drain_mid(i):
+        bytes_wait(mid_l.at[0], selfsem.at[i])
+        bytes_wait(mid_r.at[0], selfsem.at[N + 1 + i])
+
+    loop(1, N, drain_mid)
+    bytes_wait(wl.at[most, :], ssem.at[18])
+    bytes_wait(wr.at[most, :], ssem.at[19])
+    bytes_wait(rl1.at[part3], ssem.at[13])
+    bytes_wait(rr1.at[part3], ssem.at[14])
+    bytes_wait(rbl.at[part3], ssem.at[22])
+    bytes_wait(rbr.at[part3], ssem.at[23])
     part = pl.ds(0, ROWS - CAP)
     bytes_wait(gl.at[part, :], ssem.at[2])
     bytes_wait(gr.at[part, :], ssem.at[3])
@@ -565,8 +646,8 @@
     bytes_wait(bt.at[pl.ds(0, TOK - 1)], ssem.at[10])
     bytes_wait(ws.at[pl.ds(0, 3 * PIECE), :], ssem.at[11])
     bytes_wait(ws.at[pl.ds(0, 3 * PIECE), :], ssem.at[12])
-    bytes_wait(rl.at[pl.ds(0, TOK - 1)], ssem.at[15])
-    bytes_wait(rr.at[pl.ds(0, TOK - 1)], ssem.at[16])
+    bytes_wait(rl2.at[part3], ssem.at[15])
+    bytes_wait(rr2.at[part3], ssem.at[16])
 
 
 def owners(gs, xs, om):
@@ -590,14 +671,15 @@
             vm(ROWS, RANK), vm(ROWS, RANK), vm(ROWS, RANK), vm(ROWS, RANK),
             vm(TOK, RANK, wc), vm(TOK, RANK, wc), vm(TOK, RANK, wc), vm(TOK, RANK, wc),
             vm(ROWS, RANK), vm(ROWS, RANK), vm(ROWS, RANK),
-            vm(TOK, RANK, hc), vm(TOK, RANK, hc), vm(TOK, RANK, hc), vm(TOK, RANK, hc),
-            vm(TOK, RANK, hc), vm(TOK, RANK, hc),
+            vm(N, N, RANK, hc), vm(N, N, RANK, hc), vm(N, N, RANK, hc), vm(N, N, RANK, hc),
+            vm(N, RANK, hc), vm(N, RANK, hc), vm(N, RANK, hc), vm(N, RANK, hc),
+            vm(RANK, hc), vm(RANK, hc), vm(N, N, RANK, hc), vm(N, N, RANK, hc),
             vm(3, RANK, RANK), vm(3, TOK, RANK, RANK),
             vm(RANK, RANK, dtype=F32), vm(RANK, RANK, dtype=F32),
+            pltpu.SemaphoreType.DMA((24,)),
+            pltpu.SemaphoreType.DMA((24,)),
+            pltpu.SemaphoreType.DMA((6,)),
             pltpu.SemaphoreType.DMA((18,)),
-            pltpu.SemaphoreType.DMA((18,)),
-            pltpu.SemaphoreType.DMA((6,)),
-            pltpu.SemaphoreType.DMA((10,)),
         ],
         compiler_params=pltpu.CompilerParams(
             collective_id=0, has_side_effects=True, vmem_limit_bytes=58 * 1024 * 1024

time: 481 us -> 357 us (0.74)
  Pallas kernels: 474 us -> 350 us
    pallas_call x1, Pallas kernels: 447 us -> 338 us  [owners(): pl.pallas_call(functools.partial(body, float(width) ** 0.5), out_shape=ja...]
    pallas_call x1, Pallas kernels: 27 us -> 12.1 us  [sort_rows(): pl.pallas_call(sort_kernel, grid=(steps,), out_shape=(jax.ShapeDtypeStruc...]
where the time goes in v3:
time: 357 us; the launch traced here: 356 us
  Pallas kernels  350 us (98%)
  local copies, waits for them, and re-layouts  6.11 us (2%)
    pallas_call x1, Pallas kernels, owners(): pl.pallas_call(functools.partial(body, float(width) ** 0.5), out_shape=ja...  338 us
    pallas_call x1, Pallas kernels, sort_rows(): pl.pallas_call(sort_kernel, grid=(steps,), out_shape=(jax.ShapeDtypeStruc...  12.1 us

profile of v3, /device:TPU:0, one launch (start us, length us, event | category | flops | bytes accessed | tf_op | source)
XLA Modules:
  0.0 356.2 jit_solution(6571613014286373032)
XLA Ops:
  0.0 0.8 copy.7
  0.8 0.1 reshape.6.row_ids
  0.9 0.1 reshape_reshape.4.col_ids
  1.0 0.0 copy-start.1
  1.0 1.4 copy-done.1
  2.4 12.1 %sort.1 = (bf16[384,16384]{1,0:T(8,128)(2,1)}, bf16[384,6144]{1,0:T(8,128)(2,1)S(1)}) custom-call(s32[1,256]{1,0:T(1,128)S(1)} %reshape.6.row_ids, s32[256,1]{1,0:T(8,128)S(1)} %reshape_reshape.4.col_ids, bf16[128,2,16384]{2,1,0:T(2,128)(2,1)} %g_ref.1, bf16[128,6144]{1,0:T(8,128)(2,1)S(1)} %copy-done.1), custom_call_target="tpu_custom_call" | custom-call | tf_op jit(solution)/shard_map/sort/pallas_call | solution.py:67
  14.5 0.0 copy-start
  14.5 2.1 copy-done
  16.6 338.0 %owners.1 = f32[1,384,128]{2,1,0:T(8,128)} custom-call(bf16[384,16384]{1,0:T(8,128)(2,1)} %get-tuple-element.7.gs, bf16[384,6144]{1,0:T(8,128)(2,1)} %copy-done, bf16[16384,128]{1,0:T(8,128)(2,1)} %bitcast.1), custom_call_target="tpu_custom_call" | custom-call | tf_op jit(solution)/shard_map/owners/pallas_call | solution.py:663
  354.6 1.6 copy.11
Async XLA Ops:
  1.0 1.4 copy-start.1
  14.5 2.1 copy-start

commit v4 on v3

--- a/solution.py
+++ b/solution.py
@@ -32,59 +32,24 @@
     )
 
 
-def sort_kernel(row_ids, col_ids, g_ref, x_ref, gs_ref, xs_ref, pick, pick_x):
+def picks(row_ids, col_ids, pick, pick_x):
     pairs = row_ids.shape[1]
-    toks, top, hc = g_ref.shape
-
-    @pl.when(pl.program_id(0) == 0)
-    def _():
-        ids = row_ids[...]
-        same = (col_ids[...] == ids) & (
-            lax.broadcasted_iota(jnp.int32, (pairs, pairs), 0)
-            < lax.broadcasted_iota(jnp.int32, (pairs, pairs), 1)
-        )
-        rank = jnp.sum(same.astype(F32), axis=0, keepdims=True).astype(jnp.int32)
-        slot = ids * CAP + rank
-        hot = lax.broadcasted_iota(jnp.int32, (ROWS, pairs), 0) == slot
-        pick[...] = hot.astype(F32).astype(BF16)
-        token = lax.broadcasted_iota(jnp.int32, (pairs, toks), 0) - top * lax.broadcasted_iota(
-            jnp.int32, (pairs, toks), 1
-        )
-        of_token = ((token >= 0) & (token < top)).astype(F32).astype(BF16)
-        pick_x[...] = dot(pick[...], of_token).astype(BF16)
-
-    gs_ref[...] = dot(pick[...], g_ref[...].reshape(pairs, hc)).astype(BF16)
-    xs_ref[...] = dot(pick_x[...], x_ref[...]).astype(BF16)
-
-
-def sort_rows(expert_ids, out_grads, activations, steps=8):
-    toks, top = expert_ids.shape
-    pairs = toks * top
-    hidden = out_grads.shape[2]
-    width = activations.shape[1]
-    ids = expert_ids.reshape(1, pairs)
-    hc, wc = hidden // steps, width // steps
-    return pl.pallas_call(
-        sort_kernel,
-        grid=(steps,),
-        out_shape=(
-            jax.ShapeDtypeStruct((ROWS, hidden), BF16),
-            jax.ShapeDtypeStruct((ROWS, width), BF16),
-        ),
-        in_specs=[
-            pl.BlockSpec((1, pairs), lambda i: (0, 0)),
-            pl.BlockSpec((pairs, 1), lambda i: (0, 0)),
-            pl.BlockSpec((toks, top, hc), lambda i: (0, 0, i)),
-            pl.BlockSpec((toks, wc), lambda i: (0, i)),
-        ],
-        out_specs=(
-            pl.BlockSpec((ROWS, hc), lambda i: (0, i)),
-            pl.BlockSpec((ROWS, wc), lambda i: (0, i)),
-        ),
-        scratch_shapes=[pltpu.VMEM((ROWS, pairs), BF16), pltpu.VMEM((ROWS, toks), BF16)],
-        compiler_params=pltpu.CompilerParams(vmem_limit_bytes=40 * 1024 * 1024),
-        name="sort",
-    )(ids, ids.reshape(pairs, 1), out_grads, activations)
+    toks = pick_x.shape[1]
+    top = pairs // toks
+    ids = row_ids[...]
+    same = (col_ids[...] == ids) & (
+        lax.broadcasted_iota(jnp.int32, (pairs, pairs), 0)
+        < lax.broadcasted_iota(jnp.int32, (pairs, pairs), 1)
+    )
+    rank = jnp.sum(same.astype(F32), axis=0, keepdims=True).astype(jnp.int32)
+    slot = ids * CAP + rank
+    hot = lax.broadcasted_iota(jnp.int32, (ROWS, pairs), 0) == slot
+    pick[...] = hot.astype(F32).astype(BF16)
+    token = lax.broadcasted_iota(jnp.int32, (pairs, toks), 0) - top * lax.broadcasted_iota(
+        jnp.int32, (pairs, toks), 1
+    )
+    of_token = ((token >= 0) & (token < top)).astype(F32).astype(BF16)
+    pick_x[...] = dot(pick[...], of_token).astype(BF16)
 
 
 def bytes_wait(ref, sem):
@@ -128,15 +93,17 @@
 
 def body(
     scale,
-    gs, xs, om,
+    row_ids, col_ids, grads, acts, om,
     out,
+    pick, pick_x, g_in, x_in, gs, xs,
     xr, gl, gr, wl, wr,
     nls, nrs, pxl, pxr, pxl2, pxr2,
-    sp, rb, rb3, bt,
+    spa, spb, ra1, rb1, mid_a, mid_b, ra2, rb2, bta, btb,
     ws, wgl, wgr,
     pwl, pwr, rl1, rr1, mid_l, mid_r, rl2, rr2, own_rl, own_rr, rbl, rbr,
     gm, gb, cm, mm,
-    ssem, rsem, gsem, selfsem,
+    ssem, rsem, gsem, selfsem, in_sem, slot_sem, left_sem, right_sem,
+    line_send, line_recv, share_recv,
 ):
     tok = lax.axis_index("tok")
     ex = lax.axis_index("exp")
@@ -161,6 +128,31 @@
     def loop(lo, hi, fn):
         lax.fori_loop(lo, hi, lambda i, c: (fn(i), c)[1], 0)
 
+    pending = []
+
+    def later(ref, sem, when=None):
+        if when is None:
+            pending.append(lambda: bytes_wait(ref, sem))
+        else:
+            pending.append(lambda: pl.when(when)(lambda: bytes_wait(ref, sem)))
+
+    chunk = gs.shape[3]
+    chunks = half // chunk
+    pairs = pick.shape[1]
+
+    def load(side, i):
+        cols = pl.ds(pl.multiple_of(side * half + i * chunk, chunk), chunk)
+        slot = lax.rem(i, 2)
+        return pltpu.make_async_copy(
+            grads.at[:, :, cols], g_in.at[side, slot], in_sem.at[side, slot]
+        )
+
+    x_load = pltpu.make_async_copy(acts, x_in, in_sem.at[2, 0])
+    for i in range(2):
+        load(0, i).start()
+        load(1, i).start()
+    x_load.start()
+
     barrier = pltpu.get_barrier_semaphore()
 
     def greet(where):
@@ -184,6 +176,7 @@
         greet(dev(x, y, add(z, d, N), 1 - k))
 
     loop(1, N, other_core_y)
+    picks(row_ids, col_ids, pick, pick_x)
     pl.semaphore_wait(barrier, N * TOK - 1 + N + 2 * (N - 1))
 
     shift_r = lax.rem(N - z, N)
@@ -235,30 +228,55 @@
     def _():
         om_right().start()
 
+    later(wl.at[om_rows(0), :], ssem.at[0], jnp.logical_not(swap_l))
+    later(wr.at[om_rows(0), :], ssem.at[1], jnp.logical_not(swap_r))
+
     el, er = y * 2 + k, z * 2 + k
 
     def rows_of(e):
         return pl.ds(pl.multiple_of(e * CAP, CAP), CAP)
 
-    def send_g(d):
-        e = add(own_el, d, EXP)
-        remote(
-            gs.at[rows_of(e), pl.ds(0, half)], gl.at[rows_of(el), :], ssem.at[2], rsem.at[2],
-            dev(x, left_y(x, lax.div(e, 2)), z, lax.rem(e, 2)),
-        ).start()
-        e = add(own_er, d, EXP)
-        remote(
-            gs.at[rows_of(e), pl.ds(half, half)], gr.at[rows_of(er), :], ssem.at[3], rsem.at[3],
-            dev(x, y, right_z(x, lax.div(e, 2)), lax.rem(e, 2)),
-        ).start()
-
-    loop(1, EXP, send_g)
-    pltpu.make_async_copy(
-        gs.at[rows_of(own_el), pl.ds(0, half)], gl.at[rows_of(el), :], rsem.at[2]
-    ).start()
-    pltpu.make_async_copy(
-        gs.at[rows_of(own_er), pl.ds(half, half)], gr.at[rows_of(er), :], rsem.at[3]
-    ).start()
+    def send_chunk(i, first):
+        slot = lax.rem(i, 2)
+        cols = pl.ds(pl.multiple_of(i * chunk, chunk), chunk)
+        for side, dst, own, here, sems in (
+            (0, gl, own_el, el, left_sem), (1, gr, own_er, er, right_sem),
+        ):
+            load(side, i).wait()
+            if not first:
+                bytes_wait(gs.at[side, slot, part, :], slot_sem.at[side, slot])
+            block = g_in[side, slot].reshape(pairs, chunk)
+            gs[side, slot] = dot(pick[...], block).astype(BF16)
+
+            @pl.when(i + 2 < chunks)
+            def _():
+                load(side, i + 2).start()
+
+            def send_g(d):
+                e = add(own, d, EXP)
+                to, core = lax.div(e, 2), lax.rem(e, 2)
+                if side == 0:
+                    where = dev(x, left_y(x, to), z, core)
+                else:
+                    where = dev(x, y, right_z(x, to), core)
+                remote(
+                    gs.at[side, slot, rows_of(e), :], dst.at[rows_of(here), cols],
+                    slot_sem.at[side, slot], sems.at[i], where,
+                ).start()
+
+            loop(1, EXP, send_g)
+            dst[rows_of(here), cols] = gs[side, slot, rows_of(own), :]
+
+    part = pl.ds(0, ROWS - CAP)
+    send_chunk(0, True)
+
+    x_load.wait()
+
+    def sort_x(t):
+        cols = pl.ds(pl.multiple_of(t * wc, 128), wc)
+        xs[:, cols] = dot(pick_x[...], x_in[:, cols]).astype(BF16)
+
+    loop(0, TOK, sort_x)
 
     def send_x(d):
         e = add(ex, d, EXP)
@@ -267,8 +285,10 @@
         ).start()
 
     loop(1, EXP, send_x)
+    later(xr.at[part, :], ssem.at[4])
     pltpu.make_async_copy(xs.at[rows_of(ex), :], xr.at[rows_of(ex), :], rsem.at[4]).start()
 
+    send_chunk(1, True)
     bytes_wait(wl.at[om_rows(z), :], rsem.at[0])
     bytes_wait(wr.at[om_rows(y), :], rsem.at[1])
 
@@ -283,6 +303,14 @@
         ).start()
 
     loop(1, N, om_share)
+    most = pl.ds(0, 3 * quarter)
+    later(wl.at[most, :], ssem.at[18])
+    later(wr.at[most, :], ssem.at[19])
+
+    loop(2, chunks, lambda i: send_chunk(i, False))
+    for slot in range(2):
+        later(gs.at[0, slot, part, :], slot_sem.at[0, slot])
+        later(gs.at[1, slot, part, :], slot_sem.at[1, slot])
 
     def piece(i):
         return pl.ds(pl.multiple_of(i * PIECE, PIECE), PIECE)
@@ -361,65 +389,144 @@
         bytes_wait(gb.at[phase, pl.ds(0, TOK - 1)], gsem.at[2 * phase + 1])
         return inverse_factor(c, cm, mm)
 
-    def reduce_x(p, dst, s, r):
+    part3 = pl.ds(0, N - 1)
+
+    def sum_along(own, got, me, other):
+        def term(i, acc):
+            return acc + got[add(me, i, N), other].astype(F32)
+
+        return lax.fori_loop(1, N, term, own[me, other].astype(F32))
+
+    def sum_last(own, got, me):
+        def term(i, acc):
+            return acc + got[add(me, i, N)].astype(F32)
+
+        return lax.fori_loop(1, N, term, own[me].astype(F32))
+
+    def x_cols(b, c):
+        return pl.ds(pl.multiple_of((b * N + c) * wc, 128), wc)
+
+    rh = RANK // 2
+
+    def reduce_x(p, phase):
         pt = p.T.astype(BF16)
-
-        def chunk(d):
-            t = add(tok, d, TOK)
-            cols = pl.ds(pl.multiple_of(t * wc, 128), wc)
-            sp[t] = dot(pt, xr[:, cols]).astype(BF16)
-
-            @pl.when(d < TOK)
+        s, r = line_send.at[phase], line_recv.at[phase]
+        ra, rb = ra1.at[phase], rb1.at[phase]
+        ra_last, rb_last = ra2.at[phase], rb2.at[phase]
+
+        def group(d):
+            b = add(y, d, N)
+
+            def one(c):
+                v = dot(pt, xr[:, x_cols(b, c)]).astype(BF16)
+                spa[b, c] = v[:rh]
+                spb[c, b] = v[rh:]
+
+            loop(0, N, one)
+
+            @pl.when(d < N)
             def _():
-                remote(sp.at[t], dst.at[tok], s, r, (t, ex)).start()
-
-        loop(1, TOK + 1, chunk)
-        pltpu.make_async_copy(sp.at[tok], dst.at[tok], r).start()
-        bytes_wait(dst, r)
-        total = lax.fori_loop(
-            0, TOK, lambda i, c: c + dst[i].astype(F32), jnp.zeros((RANK, wc), F32)
-        )
-        bytes_wait(sp.at[pl.ds(0, TOK - 1)], s)
-        return total
-
-    kc = 1024
-
-    def g_dot(w_l, w_r):
-        def step(j, acc):
-            cols = pl.ds(pl.multiple_of(j * kc, kc), kc)
-            a, b = acc
-            return (
-                a + dot(gl[:, cols], w_l[cols, :]),
-                b + dot(gr[:, cols], w_r[cols, :]),
-            )
-
-        zero = jnp.zeros((ROWS, RANK), F32)
-        return lax.fori_loop(0, half // kc, step, (zero, zero))
-
-    most = pl.ds(0, 3 * quarter)
+                remote(spa.at[b], ra.at[y], s.at[0], r.at[0], dev(x, b, z, k)).start()
+
+        loop(1, N + 1, group)
+
+        def send_b(d):
+            c = add(z, d, N)
+            remote(spb.at[c], rb.at[z], s.at[1], r.at[1], dev(x, y, c, k)).start()
+
+        loop(1, N, send_b)
+        bytes_wait(ra.at[part3], r.at[0])
+
+        def second_a(d):
+            c = add(z, d, N)
+            mid_a[c] = sum_along(spa, ra, y, c).astype(BF16)
+
+            @pl.when(d < N)
+            def _():
+                remote(mid_a.at[c], ra_last.at[z], s.at[2], r.at[2], dev(x, y, c, k)).start()
+
+        loop(1, N + 1, second_a)
+        bytes_wait(rb.at[part3], r.at[1])
+
+        def second_b(d):
+            b = add(y, d, N)
+            mid_b[b] = sum_along(spb, rb, z, b).astype(BF16)
+
+            @pl.when(d < N)
+            def _():
+                remote(mid_b.at[b], rb_last.at[y], s.at[3], r.at[3], dev(x, b, z, k)).start()
+
+        loop(1, N + 1, second_b)
+        bytes_wait(ra_last.at[part3], r.at[2])
+        top = sum_last(mid_a, ra_last, z)
+        bytes_wait(rb_last.at[part3], r.at[3])
+        low = sum_last(mid_b, rb_last, y)
+        bytes_wait(spa.at[part3], s.at[0])
+        bytes_wait(spb.at[part3], s.at[1])
+        bytes_wait(mid_a.at[part3], s.at[2])
+        bytes_wait(mid_b.at[part3], s.at[3])
+        return jnp.concatenate([top, low], axis=0)
+
     bytes_wait(wl.at[most, :], rsem.at[18])
     bytes_wait(wr.at[most, :], rsem.at[19])
-    bytes_wait(gl, rsem.at[2])
-    bytes_wait(gr, rsem.at[3])
-    left, right = g_dot(wl, wr)
+
+    def proj_chunk(i, acc):
+        cols = pl.ds(pl.multiple_of(i * chunk, chunk), chunk)
+        a, b = acc
+        bytes_wait(gl.at[part, cols], left_sem.at[i])
+        a = a + dot(gl[:, cols], wl[cols, :])
+        bytes_wait(gr.at[part, cols], right_sem.at[i])
+        b = b + dot(gr[:, cols], wr[cols, :])
+        return a, b
+
+    zero = jnp.zeros((ROWS, RANK), F32)
+    left, right = lax.fori_loop(0, chunks, proj_chunk, (zero, zero))
     proj = to_x(left, right, pxl, pxr, 0).astype(BF16).astype(F32)
     bytes_wait(xr, rsem.at[4])
 
-    s = reduce_x(proj, rb, ssem.at[9], rsem.at[9])
+    s = reduce_x(proj, 0)
     inv = gram_all(s, 0)
-    bt[tok] = jnp.dot(inv, s, precision=HIGH, preferred_element_type=F32).astype(BF16)
-
-    def send_b(d):
-        remote(
-            bt.at[tok], bt.at[tok], ssem.at[10], rsem.at[10], (add(tok, d, TOK), ex)
-        ).start()
-
-    loop(1, TOK, send_b)
-    bytes_wait(bt.at[pl.ds(0, TOK - 1)], rsem.at[10])
+    basis = jnp.dot(inv, s, precision=HIGH, preferred_element_type=F32).astype(BF16)
+    bta[y, z] = basis[:rh]
+    btb[z, y] = basis[rh:]
+
+    def first_b(d):
+        c, b = add(z, d, N), add(y, d, N)
+        remote(
+            bta.at[y, z], bta.at[y, z], line_send.at[2, 0], line_recv.at[2, 0], dev(x, y, c, k)
+        ).start()
+        remote(
+            btb.at[z, y], btb.at[z, y], line_send.at[2, 1], line_recv.at[2, 1], dev(x, b, z, k)
+        ).start()
+
+    loop(1, N, first_b)
+    bytes_wait(bta.at[y, part3], line_recv.at[2, 0])
+
+    def then_a(d):
+        remote(
+            bta.at[y], bta.at[y], line_send.at[2, 2], line_recv.at[2, 2], dev(x, add(y, d, N), z, k)
+        ).start()
+
+    loop(1, N, then_a)
+    bytes_wait(btb.at[z, part3], line_recv.at[2, 1])
+
+    def then_b(d):
+        remote(
+            btb.at[z], btb.at[z], line_send.at[2, 3], line_recv.at[2, 3], dev(x, y, add(z, d, N), k)
+        ).start()
+
+    loop(1, N, then_b)
+    later(bta.at[0, part3], line_send.at[2, 0])
+    later(btb.at[0, part3], line_send.at[2, 1])
+    later(bta.at[part3], line_send.at[2, 2])
+    later(btb.at[part3], line_send.at[2, 3])
+    bytes_wait(bta.at[part3], line_recv.at[2, 2])
+    bytes_wait(btb.at[part3], line_recv.at[2, 3])
 
     def w_step(t, acc):
-        cols = pl.ds(pl.multiple_of(t * wc, 128), wc)
-        return acc + dot_t(xr[:, cols], bt[t])
+        b, c = lax.div(t, N), lax.rem(t, N)
+        both = jnp.concatenate([bta[b, c], btb[c, b]], axis=0)
+        return acc + dot_t(xr[:, x_cols(b, c)], both)
 
     weights = lax.fori_loop(0, TOK, w_step, jnp.zeros((ROWS, RANK), F32))
     ws[...] = weights.astype(BF16)
@@ -436,6 +543,10 @@
         ).start()
 
     loop(1, N, go_w)
+    later(ws.at[pl.ds(0, 3 * PIECE), :], ssem.at[11])
+    later(ws.at[pl.ds(0, 3 * PIECE), :], ssem.at[12])
+    later(ws.at[piece(0), :], selfsem.at[16], jnp.logical_not(swap_l))
+    later(ws.at[piece(0), :], selfsem.at[17], jnp.logical_not(swap_r))
 
     @pl.when(swap_l)
     def _():
@@ -492,18 +603,13 @@
             remote(pwr.at[g2], rr1.at[y], ssem.at[14], rsem.at[14], dev(x, g2, z, k)).start()
 
     loop(1, N + 1, power_group)
-    part3 = pl.ds(0, N - 1)
+    later(rl1.at[part3], ssem.at[13])
+    later(rr1.at[part3], ssem.at[14])
     bytes_wait(rl1.at[part3], rsem.at[13])
-
-    def sum_along(d, own, got, me, other):
-        def term(i, acc):
-            return acc + got[add(me, i, N), other].astype(F32)
-
-        return lax.fori_loop(1, N, term, own[me, other].astype(F32))
 
     def stage2_left(i):
         b = add(y, i, N)
-        mid_l[b] = sum_along(i, pwl, rl1, z, b).astype(BF16)
+        mid_l[b] = sum_along(pwl, rl1, z, b).astype(BF16)
 
         @pl.when(jnp.logical_or(i < N, jnp.logical_not(swap_l)))
         def _():
@@ -513,7 +619,7 @@
 
     def stage2_right(i):
         c = add(z, i, N)
-        mid_r[c] = sum_along(i, pwr, rr1, y, c).astype(BF16)
+        mid_r[c] = sum_along(pwr, rr1, y, c).astype(BF16)
 
         @pl.when(jnp.logical_or(i < N, jnp.logical_not(swap_r)))
         def _():
@@ -522,6 +628,9 @@
             ).start()
 
     loop(1, N + 1, stage2_left)
+    for i in range(1, N):
+        later(mid_l.at[0], selfsem.at[i])
+    later(mid_l.at[0], selfsem.at[N], jnp.logical_not(swap_l))
 
     @pl.when(swap_l)
     def _():
@@ -529,6 +638,9 @@
 
     bytes_wait(rr1.at[part3], rsem.at[14])
     loop(1, N + 1, stage2_right)
+    for i in range(1, N):
+        later(mid_r.at[0], selfsem.at[N + 1 + i])
+    later(mid_r.at[0], selfsem.at[2 * N + 1], jnp.logical_not(swap_r))
 
     @pl.when(swap_r)
     def _():
@@ -556,6 +668,10 @@
         ).start()
 
     loop(1, N, send_r)
+    later(rl2.at[part3], ssem.at[15])
+    later(rr2.at[part3], ssem.at[16])
+    later(own_rl, selfsem.at[10], jnp.logical_not(swap_l))
+    later(own_rr, selfsem.at[11], jnp.logical_not(swap_r))
 
     @pl.when(swap_l)
     def _():
@@ -577,18 +693,20 @@
 
     def share_l(d):
         remote(
-            rbl.at[z], rbl.at[z], ssem.at[22], rsem.at[22], dev(x, y, add(z, d, N), k)
+            rbl.at[z], rbl.at[z], ssem.at[22], share_recv.at[0, d], dev(x, y, add(z, d, N), k)
         ).start()
 
     loop(1, N, share_l)
+    later(rbl.at[part3], ssem.at[22])
     bytes_wait(rbr.at[y], rsem.at[16])
 
     def share_r(d):
         remote(
-            rbr.at[y], rbr.at[y], ssem.at[23], rsem.at[23], dev(x, add(y, d, N), z, k)
+            rbr.at[y], rbr.at[y], ssem.at[23], share_recv.at[1, d], dev(x, add(y, d, N), z, k)
         ).start()
 
     loop(1, N, share_r)
+    later(rbr.at[part3], ssem.at[23])
 
     def left_group(g, acc):
         return lax.fori_loop(
@@ -603,58 +721,36 @@
     zero = jnp.zeros((ROWS, RANK), F32)
     left = left_group(z, zero)
     right = right_group(y, zero)
-    bytes_wait(rbl.at[part3], rsem.at[22])
-    bytes_wait(rbr.at[part3], rsem.at[23])
-    left = lax.fori_loop(1, N, lambda d, t: left_group(add(z, d, N), t), left)
-    right = lax.fori_loop(1, N, lambda d, t: right_group(add(y, d, N), t), right)
+
+    def next_groups(d, acc):
+        a, b = acc
+        g = add(z, N - d, N)
+        bytes_wait(rbl.at[g], share_recv.at[0, d])
+        a = left_group(g, a)
+        g = add(y, N - d, N)
+        bytes_wait(rbr.at[g], share_recv.at[1, d])
+        b = right_group(g, b)
+        return a, b
+
+    left, right = lax.fori_loop(1, N, next_groups, (left, right))
     second = to_x(left, right, pxl2, pxr2, 1).astype(BF16).astype(F32)
 
-    s3 = reduce_x(second, rb3, ssem.at[17], rsem.at[17])
+    s3 = reduce_x(second, 1)
     inv = gram_all(s3, 2)
     last = jnp.dot(inv, s3, precision=HIGH, preferred_element_type=F32)
     out[0] = last.T * scale
 
-    @pl.when(jnp.logical_not(swap_l))
-    def _():
-        om_left().wait_send()
-        bytes_wait(ws.at[piece(0), :], selfsem.at[16])
-        bytes_wait(mid_l.at[0], selfsem.at[N])
-        bytes_wait(own_rl, selfsem.at[10])
-
-    @pl.when(jnp.logical_not(swap_r))
-    def _():
-        om_right().wait_send()
-        bytes_wait(ws.at[piece(0), :], selfsem.at[17])
-        bytes_wait(mid_r.at[0], selfsem.at[2 * N + 1])
-        bytes_wait(own_rr, selfsem.at[11])
-
-    def drain_mid(i):
-        bytes_wait(mid_l.at[0], selfsem.at[i])
-        bytes_wait(mid_r.at[0], selfsem.at[N + 1 + i])
-
-    loop(1, N, drain_mid)
-    bytes_wait(wl.at[most, :], ssem.at[18])
-    bytes_wait(wr.at[most, :], ssem.at[19])
-    bytes_wait(rl1.at[part3], ssem.at[13])
-    bytes_wait(rr1.at[part3], ssem.at[14])
-    bytes_wait(rbl.at[part3], ssem.at[22])
-    bytes_wait(rbr.at[part3], ssem.at[23])
-    part = pl.ds(0, ROWS - CAP)
-    bytes_wait(gl.at[part, :], ssem.at[2])
-    bytes_wait(gr.at[part, :], ssem.at[3])
-    bytes_wait(xr.at[part, :], ssem.at[4])
-    bytes_wait(bt.at[pl.ds(0, TOK - 1)], ssem.at[10])
-    bytes_wait(ws.at[pl.ds(0, 3 * PIECE), :], ssem.at[11])
-    bytes_wait(ws.at[pl.ds(0, 3 * PIECE), :], ssem.at[12])
-    bytes_wait(rl2.at[part3], ssem.at[15])
-    bytes_wait(rr2.at[part3], ssem.at[16])
-
-
-def owners(gs, xs, om):
-    hidden = gs.shape[1]
-    width = xs.shape[1]
+    for drain in pending:
+        drain()
+
+
+def owners(row_ids, col_ids, grads, acts, om):
+    toks, top, hidden = grads.shape
+    width = acts.shape[1]
     half = hidden // 2
     wc, hc = width // TOK, half // TOK
+    chunk = half // 8
+    rh = RANK // 2
 
     def vm(*shape, dtype=BF16):
         return pltpu.VMEM(shape, dtype)
@@ -663,13 +759,17 @@
     return pl.pallas_call(
         functools.partial(body, float(width) ** 0.5),
         out_shape=jax.ShapeDtypeStruct((1, wc, RANK), F32),
-        in_specs=[any_spec] * 3,
+        in_specs=[pl.BlockSpec(memory_space=pltpu.VMEM)] * 2 + [any_spec] * 3,
         out_specs=pl.BlockSpec(memory_space=pltpu.VMEM),
         scratch_shapes=[
+            vm(ROWS, toks * top), vm(ROWS, toks), vm(2, 2, toks, top, chunk), vm(toks, width),
+            vm(2, 2, ROWS, chunk), vm(ROWS, width),
             vm(ROWS, width), vm(ROWS, half), vm(ROWS, half), vm(half, RANK), vm(half, RANK),
             vm(2, ROWS, RANK), vm(2, ROWS, RANK),
             vm(ROWS, RANK), vm(ROWS, RANK), vm(ROWS, RANK), vm(ROWS, RANK),
-            vm(TOK, RANK, wc), vm(TOK, RANK, wc), vm(TOK, RANK, wc), vm(TOK, RANK, wc),
+            vm(N, N, rh, wc), vm(N, N, rh, wc), vm(2, N, N, rh, wc), vm(2, N, N, rh, wc),
+            vm(N, rh, wc), vm(N, rh, wc), vm(2, N, rh, wc), vm(2, N, rh, wc),
+            vm(N, N, rh, wc), vm(N, N, rh, wc),
             vm(ROWS, RANK), vm(ROWS, RANK), vm(ROWS, RANK),
             vm(N, N, RANK, hc), vm(N, N, RANK, hc), vm(N, N, RANK, hc), vm(N, N, RANK, hc),
             vm(N, RANK, hc), vm(N, RANK, hc), vm(N, RANK, hc), vm(N, RANK, hc),
@@ -680,18 +780,25 @@
             pltpu.SemaphoreType.DMA((24,)),
             pltpu.SemaphoreType.DMA((6,)),
             pltpu.SemaphoreType.DMA((18,)),
+            pltpu.SemaphoreType.DMA((3, 2)),
+            pltpu.SemaphoreType.DMA((2, 2)),
+            pltpu.SemaphoreType.DMA((8,)),
+            pltpu.SemaphoreType.DMA((8,)),
+            pltpu.SemaphoreType.DMA((3, 4)),
+            pltpu.SemaphoreType.DMA((3, 4)),
+            pltpu.SemaphoreType.DMA((2, N)),
         ],
         compiler_params=pltpu.CompilerParams(
-            collective_id=0, has_side_effects=True, vmem_limit_bytes=58 * 1024 * 1024
+            collective_id=0, has_side_effects=True, vmem_limit_bytes=60 * 1024 * 1024
         ),
         name="owners",
-    )(gs, xs, om)
+    )(row_ids, col_ids, grads, acts, om)
 
 
 def shards(activations, expert_ids, out_grads, sketch_matrix):
-    gs, xs = sort_rows(expert_ids, out_grads, activations)
+    ids = expert_ids.reshape(1, -1)
     om = sketch_matrix.reshape(sketch_matrix.shape[1:])
-    return owners(gs, xs, om)
+    return owners(ids, ids.reshape(-1, 1), out_grads, activations, om)
 
 
 def solution(mesh):

time: 357 us -> 329 us (0.922)
  Pallas kernels: 350 us -> 325 us
    pallas_call x1, Pallas kernels: 338 us -> 325 us  [owners(): pl.pallas_call(functools.partial(body, float(width) ** 0.5), out_shape=ja...]
    pallas_call x1 -> x0, Pallas kernels: 12.1 us -> none  [sort_rows(): pl.pallas_call(sort_kernel, grid=(steps,), out_shape=(jax.ShapeDtypeStruc...]
where the time goes in v4:
time: 329 us
  Pallas kernels  325 us (99%)
  local copies, waits for them, and re-layouts  3.86 us (1%)
    pallas_call x1, Pallas kernels, owners(): pl.pallas_call(functools.partial(body, float(width) ** 0.5), out_shape=ja...  325 us

profile of v4, /device:TPU:0, one launch (start us, length us, event | category | flops | bytes accessed | tf_op | source)
XLA Modules:
  0.0 328.5 jit_solution(9915306438245016621)
XLA Ops:
  0.0 0.8 copy.7
  0.8 0.7 reshape.6.row_ids
  1.5 0.7 reshape_reshape.4.col_ids
  2.2 324.7 %owners.1 = f32[1,384,128]{2,1,0:T(8,128)} custom-call(s32[1,256]{1,0:T(1,128)} %reshape.6.row_ids, s32[256,1]{1,0:T(8,128)} %reshape_reshape.4.col_ids, bf16[128,2,16384]{2,1,0:T(2,128)(2,1)} %grads.1, bf16[128,6144]{1,0:T(8,128)(2,1)} %acts.1, bf16[16384,128]{1,0:T(8,128)(2,1)} %bitcast.1), custom_call_target="tpu_custom_call" | custom-call | tf_op jit(solution)/shard_map/owners/pallas_call | solution.py:759
  326.9 1.6 copy.11

commit v5 on v4

--- a/solution.py
+++ b/solution.py
@@ -177,6 +177,22 @@
 
     loop(1, N, other_core_y)
     picks(row_ids, col_ids, pick, pick_x)
+    part = pl.ds(0, ROWS - CAP)
+
+    def sort_side(i, side, first):
+        slot = lax.rem(i, 2)
+        load(side, i).wait()
+        if not first:
+            bytes_wait(gs.at[side, slot, part, :], slot_sem.at[side, slot])
+        block = g_in[side, slot].reshape(pairs, chunk)
+        gs[side, slot] = dot(pick[...], block).astype(BF16)
+
+        @pl.when(i + 2 < chunks)
+        def _():
+            load(side, i + 2).start()
+
+    sort_side(0, 0, True)
+    sort_side(0, 1, True)
     pl.semaphore_wait(barrier, N * TOK - 1 + N + 2 * (N - 1))
 
     shift_r = lax.rem(N - z, N)
@@ -236,39 +252,35 @@
     def rows_of(e):
         return pl.ds(pl.multiple_of(e * CAP, CAP), CAP)
 
-    def send_chunk(i, first):
+    def send_side(i, side):
         slot = lax.rem(i, 2)
         cols = pl.ds(pl.multiple_of(i * chunk, chunk), chunk)
-        for side, dst, own, here, sems in (
-            (0, gl, own_el, el, left_sem), (1, gr, own_er, er, right_sem),
-        ):
-            load(side, i).wait()
-            if not first:
-                bytes_wait(gs.at[side, slot, part, :], slot_sem.at[side, slot])
-            block = g_in[side, slot].reshape(pairs, chunk)
-            gs[side, slot] = dot(pick[...], block).astype(BF16)
-
-            @pl.when(i + 2 < chunks)
-            def _():
-                load(side, i + 2).start()
-
-            def send_g(d):
-                e = add(own, d, EXP)
-                to, core = lax.div(e, 2), lax.rem(e, 2)
-                if side == 0:
-                    where = dev(x, left_y(x, to), z, core)
-                else:
-                    where = dev(x, y, right_z(x, to), core)
-                remote(
-                    gs.at[side, slot, rows_of(e), :], dst.at[rows_of(here), cols],
-                    slot_sem.at[side, slot], sems.at[i], where,
-                ).start()
-
-            loop(1, EXP, send_g)
-            dst[rows_of(here), cols] = gs[side, slot, rows_of(own), :]
-
-    part = pl.ds(0, ROWS - CAP)
-    send_chunk(0, True)
+        dst, own, here, sems = (
+            (gl, own_el, el, left_sem) if side == 0 else (gr, own_er, er, right_sem)
+        )
+
+        def send_g(d):
+            e = add(own, d, EXP)
+            to, core = lax.div(e, 2), lax.rem(e, 2)
+            if side == 0:
+                where = dev(x, left_y(x, to), z, core)
+            else:
+                where = dev(x, y, right_z(x, to), core)
+            remote(
+                gs.at[side, slot, rows_of(e), :], dst.at[rows_of(here), cols],
+                slot_sem.at[side, slot], sems.at[i], where,
+            ).start()
+
+        loop(1, EXP, send_g)
+        dst[rows_of(here), cols] = gs[side, slot, rows_of(own), :]
+
+    def send_chunk(i, first):
+        for side in range(2):
+            sort_side(i, side, first)
+            send_side(i, side)
+
+    send_side(0, 0)
+    send_side(0, 1)
 
     x_load.wait()
 
@@ -391,11 +403,11 @@
 
     part3 = pl.ds(0, N - 1)
 
-    def sum_along(own, got, me, other):
-        def term(i, acc):
-            return acc + got[add(me, i, N), other].astype(F32)
-
-        return lax.fori_loop(1, N, term, own[me, other].astype(F32))
+    def sum_along(own, got, me, cols):
+        total = own[me, :, cols].astype(F32)
+        for i in range(1, N):
+            total = total + got[add(me, i, N), :, cols].astype(F32)
+        return total
 
     def sum_last(own, got, me):
         def term(i, acc):
@@ -403,8 +415,10 @@
 
         return lax.fori_loop(1, N, term, own[me].astype(F32))
 
-    def x_cols(b, c):
-        return pl.ds(pl.multiple_of((b * N + c) * wc, 128), wc)
+    def span(i, n):
+        return pl.ds(pl.multiple_of(i * n, 128), n)
+
+    wg, hg = N * wc, N * hc
 
     rh = RANK // 2
 
@@ -416,13 +430,10 @@
 
         def group(d):
             b = add(y, d, N)
-
-            def one(c):
-                v = dot(pt, xr[:, x_cols(b, c)]).astype(BF16)
-                spa[b, c] = v[:rh]
-                spb[c, b] = v[rh:]
-
-            loop(0, N, one)
+            v = dot(pt, xr[:, span(b, wg)]).astype(BF16)
+            spa[b] = v[:rh]
+            for c in range(N):
+                spb[c, :, span(b, wc)] = v[rh:, c * wc : (c + 1) * wc]
 
             @pl.when(d < N)
             def _():
@@ -439,7 +450,7 @@
 
         def second_a(d):
             c = add(z, d, N)
-            mid_a[c] = sum_along(spa, ra, y, c).astype(BF16)
+            mid_a[c] = sum_along(spa, ra, y, span(c, wc)).astype(BF16)
 
             @pl.when(d < N)
             def _():
@@ -450,7 +461,7 @@
 
         def second_b(d):
             b = add(y, d, N)
-            mid_b[b] = sum_along(spb, rb, z, b).astype(BF16)
+            mid_b[b] = sum_along(spb, rb, z, span(b, wc)).astype(BF16)
 
             @pl.when(d < N)
             def _():
@@ -487,20 +498,22 @@
     s = reduce_x(proj, 0)
     inv = gram_all(s, 0)
     basis = jnp.dot(inv, s, precision=HIGH, preferred_element_type=F32).astype(BF16)
-    bta[y, z] = basis[:rh]
-    btb[z, y] = basis[rh:]
+    bta[y, :, span(z, wc)] = basis[:rh]
+    btb[z, :, span(y, wc)] = basis[rh:]
+    own_a, own_b = bta.at[y, :, span(z, wc)], btb.at[z, :, span(y, wc)]
+    three = pl.ds(0, (N - 1) * wc)
 
     def first_b(d):
         c, b = add(z, d, N), add(y, d, N)
         remote(
-            bta.at[y, z], bta.at[y, z], line_send.at[2, 0], line_recv.at[2, 0], dev(x, y, c, k)
-        ).start()
-        remote(
-            btb.at[z, y], btb.at[z, y], line_send.at[2, 1], line_recv.at[2, 1], dev(x, b, z, k)
+            own_a, own_a, line_send.at[2, 0], line_recv.at[2, 0], dev(x, y, c, k)
+        ).start()
+        remote(
+            own_b, own_b, line_send.at[2, 1], line_recv.at[2, 1], dev(x, b, z, k)
         ).start()
 
     loop(1, N, first_b)
-    bytes_wait(bta.at[y, part3], line_recv.at[2, 0])
+    bytes_wait(bta.at[y, :, three], line_recv.at[2, 0])
 
     def then_a(d):
         remote(
@@ -508,7 +521,7 @@
         ).start()
 
     loop(1, N, then_a)
-    bytes_wait(btb.at[z, part3], line_recv.at[2, 1])
+    bytes_wait(btb.at[z, :, three], line_recv.at[2, 1])
 
     def then_b(d):
         remote(
@@ -516,19 +529,19 @@
         ).start()
 
     loop(1, N, then_b)
-    later(bta.at[0, part3], line_send.at[2, 0])
-    later(btb.at[0, part3], line_send.at[2, 1])
+    later(bta.at[0, :, three], line_send.at[2, 0])
+    later(btb.at[0, :, three], line_send.at[2, 1])
     later(bta.at[part3], line_send.at[2, 2])
     later(btb.at[part3], line_send.at[2, 3])
     bytes_wait(bta.at[part3], line_recv.at[2, 2])
     bytes_wait(btb.at[part3], line_recv.at[2, 3])
 
-    def w_step(t, acc):
-        b, c = lax.div(t, N), lax.rem(t, N)
-        both = jnp.concatenate([bta[b, c], btb[c, b]], axis=0)
-        return acc + dot_t(xr[:, x_cols(b, c)], both)
-
-    weights = lax.fori_loop(0, TOK, w_step, jnp.zeros((ROWS, RANK), F32))
+    def w_step(b, acc):
+        low = jnp.concatenate([btb[c, :, span(b, wc)] for c in range(N)], axis=1)
+        both = jnp.concatenate([bta[b], low], axis=0)
+        return acc + dot_t(xr[:, span(b, wg)], both)
+
+    weights = lax.fori_loop(0, N, w_step, jnp.zeros((ROWS, RANK), F32))
     ws[...] = weights.astype(BF16)
 
     def go_w(d):
@@ -576,27 +589,16 @@
     wlt = wgl[...].astype(F32).T.astype(BF16)
     wrt = wgr[...].astype(F32).T.astype(BF16)
 
-    def cols_of(b, c):
-        return pl.ds(pl.multiple_of((b * N + c) * hc, 128), hc)
-
     def power_group(d):
         g = add(z, d, N)
-
-        def left_one(b):
-            pwl[g, b] = dot(wlt, gl[:, cols_of(b, g)]).astype(BF16)
-
-        loop(0, N, left_one)
+        pwl[g] = dot(wlt, gl[:, span(g, hg)]).astype(BF16)
 
         @pl.when(d < N)
         def _():
             remote(pwl.at[g], rl1.at[z], ssem.at[13], rsem.at[13], dev(x, y, g, k)).start()
 
         g2 = add(y, d, N)
-
-        def right_one(c):
-            pwr[g2, c] = dot(wrt, gr[:, cols_of(g2, c)]).astype(BF16)
-
-        loop(0, N, right_one)
+        pwr[g2] = dot(wrt, gr[:, span(g2, hg)]).astype(BF16)
 
         @pl.when(d < N)
         def _():
@@ -609,7 +611,7 @@
 
     def stage2_left(i):
         b = add(y, i, N)
-        mid_l[b] = sum_along(pwl, rl1, z, b).astype(BF16)
+        mid_l[b] = sum_along(pwl, rl1, z, span(b, hc)).astype(BF16)
 
         @pl.when(jnp.logical_or(i < N, jnp.logical_not(swap_l)))
         def _():
@@ -619,7 +621,7 @@
 
     def stage2_right(i):
         c = add(z, i, N)
-        mid_r[c] = sum_along(pwr, rr1, y, c).astype(BF16)
+        mid_r[c] = sum_along(pwr, rr1, y, span(c, hc)).astype(BF16)
 
         @pl.when(jnp.logical_or(i < N, jnp.logical_not(swap_r)))
         def _():
@@ -658,13 +660,15 @@
     own_rl[...] = right_basis[:, :hc]
     own_rr[...] = right_basis[:, hc:]
 
+    at_l, at_r = rbl.at[z, :, span(y, hc)], rbr.at[y, :, span(z, hc)]
+
     def send_r(d):
         a = add(x, d, N)
         remote(
-            own_rl, rbl.at[z, y], ssem.at[15], rsem.at[15], dev(a, left_y(a, x), z, k)
-        ).start()
-        remote(
-            own_rr, rbr.at[y, z], ssem.at[16], rsem.at[16], dev(a, y, right_z(a, x), k)
+            own_rl, at_l, ssem.at[15], rsem.at[15], dev(a, left_y(a, x), z, k)
+        ).start()
+        remote(
+            own_rr, at_r, ssem.at[16], rsem.at[16], dev(a, y, right_z(a, x), k)
         ).start()
 
     loop(1, N, send_r)
@@ -675,19 +679,19 @@
 
     @pl.when(swap_l)
     def _():
-        pltpu.make_async_copy(own_rl, rbl.at[z, y], rsem.at[15]).start()
+        pltpu.make_async_copy(own_rl, at_l, rsem.at[15]).start()
 
     @pl.when(jnp.logical_not(swap_l))
     def _():
-        remote(own_rl, rbl.at[z, y], selfsem.at[10], rsem.at[15], dev(x, 0, z, k)).start()
+        remote(own_rl, at_l, selfsem.at[10], rsem.at[15], dev(x, 0, z, k)).start()
 
     @pl.when(swap_r)
     def _():
-        pltpu.make_async_copy(own_rr, rbr.at[y, z], rsem.at[16]).start()
+        pltpu.make_async_copy(own_rr, at_r, rsem.at[16]).start()
 
     @pl.when(jnp.logical_not(swap_r))
     def _():
-        remote(own_rr, rbr.at[y, z], selfsem.at[11], rsem.at[16], dev(x, y, 0, k)).start()
+        remote(own_rr, at_r, selfsem.at[11], rsem.at[16], dev(x, y, 0, k)).start()
 
     bytes_wait(rbl.at[z], rsem.at[15])
 
@@ -709,14 +713,10 @@
     later(rbr.at[part3], ssem.at[23])
 
     def left_group(g, acc):
-        return lax.fori_loop(
-            0, N, lambda b, t: t + dot_t(gl[:, cols_of(b, g)], rbl[g, b]), acc
-        )
+        return acc + dot_t(gl[:, span(g, hg)], rbl[g])
 
     def right_group(g, acc):
-        return lax.fori_loop(
-            0, N, lambda c, t: t + dot_t(gr[:, cols_of(g, c)], rbr[g, c]), acc
-        )
+        return acc + dot_t(gr[:, span(g, hg)], rbr[g])
 
     zero = jnp.zeros((ROWS, RANK), F32)
     left = left_group(z, zero)
@@ -767,13 +767,13 @@
             vm(ROWS, width), vm(ROWS, half), vm(ROWS, half), vm(half, RANK), vm(half, RANK),
             vm(2, ROWS, RANK), vm(2, ROWS, RANK),
             vm(ROWS, RANK), vm(ROWS, RANK), vm(ROWS, RANK), vm(ROWS, RANK),
-            vm(N, N, rh, wc), vm(N, N, rh, wc), vm(2, N, N, rh, wc), vm(2, N, N, rh, wc),
+            vm(N, rh, N * wc), vm(N, rh, N * wc), vm(2, N, rh, N * wc), vm(2, N, rh, N * wc),
             vm(N, rh, wc), vm(N, rh, wc), vm(2, N, rh, wc), vm(2, N, rh, wc),
-            vm(N, N, rh, wc), vm(N, N, rh, wc),
+            vm(N, rh, N * wc), vm(N, rh, N * wc),
             vm(ROWS, RANK), vm(ROWS, RANK), vm(ROWS, RANK),
-            vm(N, N, RANK, hc), vm(N, N, RANK, hc), vm(N, N, RANK, hc), vm(N, N, RANK, hc),
+            vm(N, RANK, N * hc), vm(N, RANK, N * hc), vm(N, RANK, N * hc), vm(N, RANK, N * hc),
             vm(N, RANK, hc), vm(N, RANK, hc), vm(N, RANK, hc), vm(N, RANK, hc),
-            vm(RANK, hc), vm(RANK, hc), vm(N, N, RANK, hc), vm(N, N, RANK, hc),
+            vm(RANK, hc), vm(RANK, hc), vm(N, RANK, N * hc), vm(N, RANK, N * hc),
             vm(3, RANK, RANK), vm(3, TOK, RANK, RANK),
             vm(RANK, RANK, dtype=F32), vm(RANK, RANK, dtype=F32),
             pltpu.SemaphoreType.DMA((24,)),

time: 329 us -> 319 us (0.970)
  Pallas kernels: 325 us -> 315 us
    pallas_call x1, Pallas kernels: 325 us -> 315 us  [owners(): pl.pallas_call(functools.partial(body, float(width) ** 0.5), out_shape=ja...]
where the time goes in v5:
time: 319 us
  Pallas kernels  315 us (99%)
  local copies, waits for them, and re-layouts  3.86 us (1%)
    pallas_call x1, Pallas kernels, owners(): pl.pallas_call(functools.partial(body, float(width) ** 0.5), out_shape=ja...  315 us

profile of v5, /device:TPU:0, one launch (start us, length us, event | category | flops | bytes accessed | tf_op | source)
XLA Modules:
  0.0 318.8 jit_solution(15424523410837237978)
XLA Ops:
  0.0 0.8 copy.7
  0.8 0.7 reshape.6.row_ids
  1.5 0.7 reshape_reshape.4.col_ids
  2.2 314.9 %owners.1 = f32[1,384,128]{2,1,0:T(8,128)} custom-call(s32[1,256]{1,0:T(1,128)} %reshape.6.row_ids, s32[256,1]{1,0:T(8,128)} %reshape_reshape.4.col_ids, bf16[128,2,16384]{2,1,0:T(2,128)(2,1)} %grads.1, bf16[128,6144]{1,0:T(8,128)(2,1)} %acts.1, bf16[16384,128]{1,0:T(8,128)(2,1)} %bitcast.1), custom_call_target="tpu_custom_call" | custom-call | tf_op jit(solution)/shard_map/owners/pallas_call | solution.py:759
  317.1 1.6 copy.11

commit v6 on v5

--- a/solution.py
+++ b/solution.py
@@ -56,6 +56,13 @@
     pltpu.make_async_copy(ref, ref, sem).wait()
 
 
+def terms(v):
+    high = v.astype(BF16)
+    rest = v - high.astype(F32)
+    mid = rest.astype(BF16)
+    return high, mid, (rest - mid.astype(F32)).astype(BF16)
+
+
 def inverse_factor(c, cm, mm):
     cm[...] = c
     rows = lax.broadcasted_iota(jnp.int32, (RANK, RANK), 0)
@@ -80,8 +87,12 @@
         mm[pl.ds(base, PANEL), :] = m
         left = jnp.where(pcol >= base + PANEL, a, 0.0)
         both = jnp.concatenate([a, m], axis=1)
+        a_high, a_mid, a_low = terms(left)
+        b_high, b_mid, b_low = terms(both)
+        deep_a = jnp.concatenate([a_high, a_high, a_mid, a_high, a_low, a_mid], axis=0)
+        deep_b = jnp.concatenate([b_high, b_mid, b_high, b_low, b_high, b_mid], axis=0)
         change = lax.dot_general(
-            left, both, (((0,), (0,)), ((), ())), precision=HIGH, preferred_element_type=F32
+            deep_a, deep_b, (((0,), (0,)), ((), ())), preferred_element_type=F32
         )
         cm[...] -= change[:, :RANK]
         mm[...] -= change[:, RANK:]
@@ -95,15 +106,15 @@
     scale,
     row_ids, col_ids, grads, acts, om,
     out,
-    pick, pick_x, g_in, x_in, gs, xs,
+    pick, pick_x, g_in, gs, xs,
     xr, gl, gr, wl, wr,
     nls, nrs, pxl, pxr, pxl2, pxr2,
     spa, spb, ra1, rb1, mid_a, mid_b, ra2, rb2, bta, btb,
     ws, wgl, wgr,
-    pwl, pwr, rl1, rr1, mid_l, mid_r, rl2, rr2, own_rl, own_rr, rbl, rbr,
+    pwl, pwr, rl1, rr1, mid_l, mid_r, turn_l, turn_r, rl2, rr2, own_rl, own_rr, rbl, rbr,
     gm, gb, cm, mm,
     ssem, rsem, gsem, selfsem, in_sem, slot_sem, left_sem, right_sem,
-    line_send, line_recv, share_recv,
+    line_send, line_recv, share_recv, piece_recv,
 ):
     tok = lax.axis_index("tok")
     ex = lax.axis_index("exp")
@@ -147,11 +158,18 @@
             grads.at[:, :, cols], g_in.at[side, slot], in_sem.at[side, slot]
         )
 
-    x_load = pltpu.make_async_copy(acts, x_in, in_sem.at[2, 0])
+    x_block = pwl.shape[2]
+    x_blocks = width // x_block
+
+    def load_x(i):
+        cols = pl.ds(i * x_block, x_block)
+        return pltpu.make_async_copy(acts.at[:, cols], pwl.at[i], in_sem.at[2, i])
+
     for i in range(2):
         load(0, i).start()
         load(1, i).start()
-    x_load.start()
+    for i in range(x_blocks):
+        load_x(i).start()
 
     barrier = pltpu.get_barrier_semaphore()
 
@@ -282,13 +300,9 @@
     send_side(0, 0)
     send_side(0, 1)
 
-    x_load.wait()
-
-    def sort_x(t):
-        cols = pl.ds(pl.multiple_of(t * wc, 128), wc)
-        xs[:, cols] = dot(pick_x[...], x_in[:, cols]).astype(BF16)
-
-    loop(0, TOK, sort_x)
+    for i in range(x_blocks):
+        load_x(i).wait()
+        xs[:, pl.ds(i * x_block, x_block)] = dot(pick_x[...], pwl[i]).astype(BF16)
 
     def send_x(d):
         e = add(ex, d, EXP)
@@ -301,6 +315,7 @@
     pltpu.make_async_copy(xs.at[rows_of(ex), :], xr.at[rows_of(ex), :], rsem.at[4]).start()
 
     send_chunk(1, True)
+    loop(2, chunks // 2, lambda i: send_chunk(i, False))
     bytes_wait(wl.at[om_rows(z), :], rsem.at[0])
     bytes_wait(wr.at[om_rows(y), :], rsem.at[1])
 
@@ -318,8 +333,7 @@
     most = pl.ds(0, 3 * quarter)
     later(wl.at[most, :], ssem.at[18])
     later(wr.at[most, :], ssem.at[19])
-
-    loop(2, chunks, lambda i: send_chunk(i, False))
+    loop(chunks // 2, chunks, lambda i: send_chunk(i, False))
     for slot in range(2):
         later(gs.at[0, slot, part, :], slot_sem.at[0, slot])
         later(gs.at[1, slot, part, :], slot_sem.at[1, slot])
@@ -613,43 +627,51 @@
         b = add(y, i, N)
         mid_l[b] = sum_along(pwl, rl1, z, span(b, hc)).astype(BF16)
 
-        @pl.when(jnp.logical_or(i < N, jnp.logical_not(swap_l)))
+        @pl.when(i < N)
         def _():
             remote(
-                mid_l.at[b], rl2.at[x], selfsem.at[i], rsem.at[20], dev(xl, b, z, k)
+                mid_l.at[b], turn_l.at[y], ssem.at[20], rsem.at[20], dev(x, b, z, k)
             ).start()
 
     def stage2_right(i):
         c = add(z, i, N)
         mid_r[c] = sum_along(pwr, rr1, y, span(c, hc)).astype(BF16)
 
-        @pl.when(jnp.logical_or(i < N, jnp.logical_not(swap_r)))
+        @pl.when(i < N)
         def _():
             remote(
-                mid_r.at[c], rr2.at[x], selfsem.at[N + 1 + i], rsem.at[21], dev(xd, y, c, k)
+                mid_r.at[c], turn_r.at[z], ssem.at[21], rsem.at[21], dev(x, y, c, k)
             ).start()
 
     loop(1, N + 1, stage2_left)
-    for i in range(1, N):
-        later(mid_l.at[0], selfsem.at[i])
-    later(mid_l.at[0], selfsem.at[N], jnp.logical_not(swap_l))
-
-    @pl.when(swap_l)
-    def _():
-        pltpu.make_async_copy(mid_l.at[y], rl2.at[x], rsem.at[20]).start()
-
+    turn_l[y] = mid_l[y]
+    later(mid_l.at[part3], ssem.at[20])
     bytes_wait(rr1.at[part3], rsem.at[14])
     loop(1, N + 1, stage2_right)
-    for i in range(1, N):
-        later(mid_r.at[0], selfsem.at[N + 1 + i])
-    later(mid_r.at[0], selfsem.at[2 * N + 1], jnp.logical_not(swap_r))
-
-    @pl.when(swap_r)
-    def _():
-        pltpu.make_async_copy(mid_r.at[z], rr2.at[x], rsem.at[21]).start()
-
-    bytes_wait(rl2, rsem.at[20])
-    bytes_wait(rr2, rsem.at[21])
+    turn_r[z] = mid_r[z]
+    later(mid_r.at[part3], ssem.at[21])
+    bytes_wait(turn_l.at[part3], rsem.at[20])
+
+    def along_x_left(i):
+        remote(
+            turn_l.at[i], rl2.at[x], selfsem.at[0], rsem.at[24], dev(add(x, i, N), y, z, k)
+        ).start()
+
+    loop(1, N, along_x_left)
+    rl2[x] = turn_l[0]
+    later(rl2.at[part3], selfsem.at[0])
+    bytes_wait(turn_r.at[part3], rsem.at[21])
+
+    def along_x_right(i):
+        remote(
+            turn_r.at[i], rr2.at[x], selfsem.at[1], rsem.at[25], dev(add(x, N - i, N), y, z, k)
+        ).start()
+
+    loop(1, N, along_x_right)
+    rr2[x] = turn_r[0]
+    later(rr2.at[part3], selfsem.at[1])
+    bytes_wait(rl2.at[part3], rsem.at[24])
+    bytes_wait(rr2.at[part3], rsem.at[25])
     zero = jnp.zeros((RANK, hc), F32)
     sl = lax.fori_loop(0, N, lambda i, c: c + rl2[i].astype(F32), zero)
     sr = lax.fori_loop(0, N, lambda i, c: c + rr2[i].astype(F32), zero)
@@ -665,10 +687,10 @@
     def send_r(d):
         a = add(x, d, N)
         remote(
-            own_rl, at_l, ssem.at[15], rsem.at[15], dev(a, left_y(a, x), z, k)
-        ).start()
-        remote(
-            own_rr, at_r, ssem.at[16], rsem.at[16], dev(a, y, right_z(a, x), k)
+            own_rl, at_l, ssem.at[15], piece_recv.at[0, y], dev(a, left_y(a, x), z, k)
+        ).start()
+        remote(
+            own_rr, at_r, ssem.at[16], piece_recv.at[1, z], dev(a, y, right_z(a, x), k)
         ).start()
 
     loop(1, N, send_r)
@@ -679,37 +701,44 @@
 
     @pl.when(swap_l)
     def _():
-        pltpu.make_async_copy(own_rl, at_l, rsem.at[15]).start()
+        pltpu.make_async_copy(own_rl, at_l, piece_recv.at[0, y]).start()
 
     @pl.when(jnp.logical_not(swap_l))
     def _():
-        remote(own_rl, at_l, selfsem.at[10], rsem.at[15], dev(x, 0, z, k)).start()
+        remote(own_rl, at_l, selfsem.at[10], piece_recv.at[0, y], dev(x, 0, z, k)).start()
 
     @pl.when(swap_r)
     def _():
-        pltpu.make_async_copy(own_rr, at_r, rsem.at[16]).start()
+        pltpu.make_async_copy(own_rr, at_r, piece_recv.at[1, z]).start()
 
     @pl.when(jnp.logical_not(swap_r))
     def _():
-        remote(own_rr, at_r, selfsem.at[11], rsem.at[16], dev(x, y, 0, k)).start()
-
-    bytes_wait(rbl.at[z], rsem.at[15])
-
-    def share_l(d):
-        remote(
-            rbl.at[z], rbl.at[z], ssem.at[22], share_recv.at[0, d], dev(x, y, add(z, d, N), k)
-        ).start()
-
-    loop(1, N, share_l)
+        remote(own_rr, at_r, selfsem.at[11], piece_recv.at[1, z], dev(x, y, 0, k)).start()
+
+    def forward(i):
+        b, c = add(y, i, N), add(z, i, N)
+        left_piece = rbl.at[z, :, span(b, hc)]
+        right_piece = rbr.at[y, :, span(c, hc)]
+        bytes_wait(left_piece, piece_recv.at[0, b])
+
+        def share_l(d):
+            remote(
+                left_piece, left_piece, ssem.at[22], share_recv.at[0, d], dev(x, y, add(z, d, N), k)
+            ).start()
+
+        loop(1, N, share_l)
+        bytes_wait(right_piece, piece_recv.at[1, c])
+
+        def share_r(d):
+            remote(
+                right_piece, right_piece, ssem.at[23], share_recv.at[1, d],
+                dev(x, add(y, d, N), z, k),
+            ).start()
+
+        loop(1, N, share_r)
+
+    loop(0, N, forward)
     later(rbl.at[part3], ssem.at[22])
-    bytes_wait(rbr.at[y], rsem.at[16])
-
-    def share_r(d):
-        remote(
-            rbr.at[y], rbr.at[y], ssem.at[23], share_recv.at[1, d], dev(x, add(y, d, N), z, k)
-        ).start()
-
-    loop(1, N, share_r)
     later(rbr.at[part3], ssem.at[23])
 
     def left_group(g, acc):
@@ -762,7 +791,7 @@
         in_specs=[pl.BlockSpec(memory_space=pltpu.VMEM)] * 2 + [any_spec] * 3,
         out_specs=pl.BlockSpec(memory_space=pltpu.VMEM),
         scratch_shapes=[
-            vm(ROWS, toks * top), vm(ROWS, toks), vm(2, 2, toks, top, chunk), vm(toks, width),
+            vm(ROWS, toks * top), vm(ROWS, toks), vm(2, 2, toks, top, chunk),
             vm(2, 2, ROWS, chunk), vm(ROWS, width),
             vm(ROWS, width), vm(ROWS, half), vm(ROWS, half), vm(half, RANK), vm(half, RANK),
             vm(2, ROWS, RANK), vm(2, ROWS, RANK),
@@ -773,19 +802,21 @@
             vm(ROWS, RANK), vm(ROWS, RANK), vm(ROWS, RANK),
             vm(N, RANK, N * hc), vm(N, RANK, N * hc), vm(N, RANK, N * hc), vm(N, RANK, N * hc),
             vm(N, RANK, hc), vm(N, RANK, hc), vm(N, RANK, hc), vm(N, RANK, hc),
+            vm(N, RANK, hc), vm(N, RANK, hc),
             vm(RANK, hc), vm(RANK, hc), vm(N, RANK, N * hc), vm(N, RANK, N * hc),
             vm(3, RANK, RANK), vm(3, TOK, RANK, RANK),
             vm(RANK, RANK, dtype=F32), vm(RANK, RANK, dtype=F32),
             pltpu.SemaphoreType.DMA((24,)),
-            pltpu.SemaphoreType.DMA((24,)),
+            pltpu.SemaphoreType.DMA((26,)),
             pltpu.SemaphoreType.DMA((6,)),
             pltpu.SemaphoreType.DMA((18,)),
-            pltpu.SemaphoreType.DMA((3, 2)),
+            pltpu.SemaphoreType.DMA((3, N)),
             pltpu.SemaphoreType.DMA((2, 2)),
             pltpu.SemaphoreType.DMA((8,)),
             pltpu.SemaphoreType.DMA((8,)),
             pltpu.SemaphoreType.DMA((3, 4)),
             pltpu.SemaphoreType.DMA((3, 4)),
+            pltpu.SemaphoreType.DMA((2, N)),
             pltpu.SemaphoreType.DMA((2, N)),
         ],
         compiler_params=pltpu.CompilerParams(

time: 319 us -> 302 us (0.947)
  Pallas kernels: 315 us -> 298 us
    pallas_call x1, Pallas kernels: 315 us -> 298 us  [owners(): pl.pallas_call(functools.partial(body, float(width) ** 0.5), out_shape=ja...]
where the time goes in v6:
time: 302 us
  Pallas kernels  298 us (99%)
  local copies, waits for them, and re-layouts  3.86 us (1%)
    pallas_call x1, Pallas kernels, owners(): pl.pallas_call(functools.partial(body, float(width) ** 0.5), out_shape=ja...  298 us

profile of v6, /device:TPU:0, one launch (start us, length us, event | category | flops | bytes accessed | tf_op | source)
XLA Modules:
  0.0 302.2 jit_solution(7446045970453784167)
XLA Ops:
  0.0 0.8 copy.7
  0.8 0.7 reshape.6.row_ids
  1.5 0.7 reshape_reshape.4.col_ids
  2.2 298.4 %owners.1 = f32[1,384,128]{2,1,0:T(8,128)} custom-call(s32[1,256]{1,0:T(1,128)} %reshape.6.row_ids, s32[256,1]{1,0:T(8,128)} %reshape_reshape.4.col_ids, bf16[128,2,16384]{2,1,0:T(2,128)(2,1)} %grads.1, bf16[128,6144]{1,0:T(8,128)(2,1)} %acts.1, bf16[16384,128]{1,0:T(8,128)(2,1)} %bitcast.1), custom_call_target="tpu_custom_call" | custom-call | tf_op jit(solution)/shard_map/owners/pallas_call | solution.py:788
  300.6 1.6 copy.11

commit v7 on v6

--- a/solution.py
+++ b/solution.py
@@ -114,7 +114,7 @@
     pwl, pwr, rl1, rr1, mid_l, mid_r, turn_l, turn_r, rl2, rr2, own_rl, own_rr, rbl, rbr,
     gm, gb, cm, mm,
     ssem, rsem, gsem, selfsem, in_sem, slot_sem, left_sem, right_sem,
-    line_send, line_recv, share_recv, piece_recv,
+    line_send, line_recv, share_recv, piece_recv, half_send, half_recv,
 ):
     tok = lax.axis_index("tok")
     ex = lax.axis_index("exp")
@@ -417,10 +417,10 @@
 
     part3 = pl.ds(0, N - 1)
 
-    def sum_along(own, got, me, cols):
-        total = own[me, :, cols].astype(F32)
+    def sum_along(own, got, me, cols, rows=slice(None)):
+        total = own[me, rows, cols].astype(F32)
         for i in range(1, N):
-            total = total + got[add(me, i, N), :, cols].astype(F32)
+            total = total + got[add(me, i, N), rows, cols].astype(F32)
         return total
 
     def sum_last(own, got, me):
@@ -603,75 +603,104 @@
     wlt = wgl[...].astype(F32).T.astype(BF16)
     wrt = wgr[...].astype(F32).T.astype(BF16)
 
+    rank_halves = (pl.ds(0, rh), pl.ds(rh, rh))
+
+    def first_left(g, h):
+        rows = rank_halves[h]
+        remote(
+            pwl.at[g, rows], rl1.at[z, rows], half_send.at[0, h], half_recv.at[0, h],
+            dev(x, y, g, k),
+        ).start()
+
+    def first_right(g, h):
+        rows = rank_halves[h]
+        remote(
+            pwr.at[g, rows], rr1.at[y, rows], half_send.at[1, h], half_recv.at[1, h],
+            dev(x, g, z, k),
+        ).start()
+
     def power_group(d):
-        g = add(z, d, N)
+        g, g2 = add(z, d, N), add(y, d, N)
         pwl[g] = dot(wlt, gl[:, span(g, hg)]).astype(BF16)
 
         @pl.when(d < N)
         def _():
-            remote(pwl.at[g], rl1.at[z], ssem.at[13], rsem.at[13], dev(x, y, g, k)).start()
-
-        g2 = add(y, d, N)
+            first_left(g, 0)
+
         pwr[g2] = dot(wrt, gr[:, span(g2, hg)]).astype(BF16)
 
         @pl.when(d < N)
         def _():
-            remote(pwr.at[g2], rr1.at[y], ssem.at[14], rsem.at[14], dev(x, g2, z, k)).start()
+            first_right(g2, 0)
 
     loop(1, N + 1, power_group)
-    later(rl1.at[part3], ssem.at[13])
-    later(rr1.at[part3], ssem.at[14])
-    bytes_wait(rl1.at[part3], rsem.at[13])
-
-    def stage2_left(i):
-        b = add(y, i, N)
-        mid_l[b] = sum_along(pwl, rl1, z, span(b, hc)).astype(BF16)
-
-        @pl.when(i < N)
-        def _():
+
+    def other_half(d):
+        first_left(add(z, d, N), 1)
+        first_right(add(y, d, N), 1)
+
+    loop(1, N, other_half)
+
+    for h in range(2):
+        rows = rank_halves[h]
+        s_h = [half_send.at[i, h] for i in range(6)]
+        r_h = [half_recv.at[i, h] for i in range(6)]
+        later(rl1.at[part3, rows], s_h[0])
+        later(rr1.at[part3, rows], s_h[1])
+
+        def stage2_left(i):
+            b = add(y, i, N)
+            mid_l[b, rows] = sum_along(pwl, rl1, z, span(b, hc), rows).astype(BF16)
+
+            @pl.when(i < N)
+            def _():
+                remote(
+                    mid_l.at[b, rows], turn_l.at[y, rows], s_h[2], r_h[2], dev(x, b, z, k)
+                ).start()
+
+        def stage2_right(i):
+            c = add(z, i, N)
+            mid_r[c, rows] = sum_along(pwr, rr1, y, span(c, hc), rows).astype(BF16)
+
+            @pl.when(i < N)
+            def _():
+                remote(
+                    mid_r.at[c, rows], turn_r.at[z, rows], s_h[3], r_h[3], dev(x, y, c, k)
+                ).start()
+
+        bytes_wait(rl1.at[part3, rows], r_h[0])
+        loop(1, N + 1, stage2_left)
+        turn_l[y, rows] = mid_l[y, rows]
+        bytes_wait(rr1.at[part3, rows], r_h[1])
+        loop(1, N + 1, stage2_right)
+        turn_r[z, rows] = mid_r[z, rows]
+
+        def along_x_left(i):
             remote(
-                mid_l.at[b], turn_l.at[y], ssem.at[20], rsem.at[20], dev(x, b, z, k)
+                turn_l.at[i, rows], rl2.at[x, rows], s_h[4], r_h[4], dev(add(x, i, N), y, z, k)
             ).start()
 
-    def stage2_right(i):
-        c = add(z, i, N)
-        mid_r[c] = sum_along(pwr, rr1, y, span(c, hc)).astype(BF16)
-
-        @pl.when(i < N)
-        def _():
+        def along_x_right(i):
             remote(
-                mid_r.at[c], turn_r.at[z], ssem.at[21], rsem.at[21], dev(x, y, c, k)
+                turn_r.at[i, rows], rr2.at[x, rows], s_h[5], r_h[5], dev(add(x, N - i, N), y, z, k)
             ).start()
 
-    loop(1, N + 1, stage2_left)
-    turn_l[y] = mid_l[y]
-    later(mid_l.at[part3], ssem.at[20])
-    bytes_wait(rr1.at[part3], rsem.at[14])
-    loop(1, N + 1, stage2_right)
-    turn_r[z] = mid_r[z]
-    later(mid_r.at[part3], ssem.at[21])
-    bytes_wait(turn_l.at[part3], rsem.at[20])
-
-    def along_x_left(i):
-        remote(
-            turn_l.at[i], rl2.at[x], selfsem.at[0], rsem.at[24], dev(add(x, i, N), y, z, k)
-        ).start()
-
-    loop(1, N, along_x_left)
-    rl2[x] = turn_l[0]
-    later(rl2.at[part3], selfsem.at[0])
-    bytes_wait(turn_r.at[part3], rsem.at[21])
-
-    def along_x_right(i):
-        remote(
-            turn_r.at[i], rr2.at[x], selfsem.at[1], rsem.at[25], dev(add(x, N - i, N), y, z, k)
-        ).start()
-
-    loop(1, N, along_x_right)
-    rr2[x] = turn_r[0]
-    later(rr2.at[part3], selfsem.at[1])
-    bytes_wait(rl2.at[part3], rsem.at[24])
-    bytes_wait(rr2.at[part3], rsem.at[25])
+        bytes_wait(turn_l.at[part3, rows], r_h[2])
+        loop(1, N, along_x_left)
+        rl2[x, rows] = turn_l[0, rows]
+        bytes_wait(turn_r.at[part3, rows], r_h[3])
+        loop(1, N, along_x_right)
+        rr2[x, rows] = turn_r[0, rows]
+        later(mid_l.at[part3, rows], s_h[2])
+        later(mid_r.at[part3, rows], s_h[3])
+        later(rl2.at[part3, rows], s_h[4])
+        later(rr2.at[part3, rows], s_h[5])
+
+    for h in range(2):
+        rows = rank_halves[h]
+        bytes_wait(rl2.at[part3, rows], half_recv.at[4, h])
+        bytes_wait(rr2.at[part3, rows], half_recv.at[5, h])
+
     zero = jnp.zeros((RANK, hc), F32)
     sl = lax.fori_loop(0, N, lambda i, c: c + rl2[i].astype(F32), zero)
     sr = lax.fori_loop(0, N, lambda i, c: c + rr2[i].astype(F32), zero)
@@ -682,62 +711,72 @@
     own_rl[...] = right_basis[:, :hc]
     own_rr[...] = right_basis[:, hc:]
 
-    at_l, at_r = rbl.at[z, :, span(y, hc)], rbr.at[y, :, span(z, hc)]
-
-    def send_r(d):
-        a = add(x, d, N)
-        remote(
-            own_rl, at_l, ssem.at[15], piece_recv.at[0, y], dev(a, left_y(a, x), z, k)
-        ).start()
-        remote(
-            own_rr, at_r, ssem.at[16], piece_recv.at[1, z], dev(a, y, right_z(a, x), k)
-        ).start()
-
-    loop(1, N, send_r)
+    def send_half(h):
+        rows = rank_halves[h]
+        from_l, from_r = own_rl.at[rows], own_rr.at[rows]
+        at_l, at_r = rbl.at[z, rows, span(y, hc)], rbr.at[y, rows, span(z, hc)]
+        here_l, here_r = piece_recv.at[0, h, y], piece_recv.at[1, h, z]
+
+        def send_r(d):
+            a = add(x, d, N)
+            remote(from_l, at_l, ssem.at[15], here_l, dev(a, left_y(a, x), z, k)).start()
+            remote(from_r, at_r, ssem.at[16], here_r, dev(a, y, right_z(a, x), k)).start()
+
+        loop(1, N, send_r)
+
+        @pl.when(swap_l)
+        def _():
+            pltpu.make_async_copy(from_l, at_l, here_l).start()
+
+        @pl.when(jnp.logical_not(swap_l))
+        def _():
+            remote(from_l, at_l, selfsem.at[10], here_l, dev(x, 0, z, k)).start()
+
+        @pl.when(swap_r)
+        def _():
+            pltpu.make_async_copy(from_r, at_r, here_r).start()
+
+        @pl.when(jnp.logical_not(swap_r))
+        def _():
+            remote(from_r, at_r, selfsem.at[11], here_r, dev(x, y, 0, k)).start()
+
+    send_half(0)
+    send_half(1)
     later(rl2.at[part3], ssem.at[15])
     later(rr2.at[part3], ssem.at[16])
     later(own_rl, selfsem.at[10], jnp.logical_not(swap_l))
     later(own_rr, selfsem.at[11], jnp.logical_not(swap_r))
 
-    @pl.when(swap_l)
-    def _():
-        pltpu.make_async_copy(own_rl, at_l, piece_recv.at[0, y]).start()
-
-    @pl.when(jnp.logical_not(swap_l))
-    def _():
-        remote(own_rl, at_l, selfsem.at[10], piece_recv.at[0, y], dev(x, 0, z, k)).start()
-
-    @pl.when(swap_r)
-    def _():
-        pltpu.make_async_copy(own_rr, at_r, piece_recv.at[1, z]).start()
-
-    @pl.when(jnp.logical_not(swap_r))
-    def _():
-        remote(own_rr, at_r, selfsem.at[11], piece_recv.at[1, z], dev(x, y, 0, k)).start()
-
-    def forward(i):
-        b, c = add(y, i, N), add(z, i, N)
-        left_piece = rbl.at[z, :, span(b, hc)]
-        right_piece = rbr.at[y, :, span(c, hc)]
-        bytes_wait(left_piece, piece_recv.at[0, b])
-
-        def share_l(d):
-            remote(
-                left_piece, left_piece, ssem.at[22], share_recv.at[0, d], dev(x, y, add(z, d, N), k)
-            ).start()
-
-        loop(1, N, share_l)
-        bytes_wait(right_piece, piece_recv.at[1, c])
-
-        def share_r(d):
-            remote(
-                right_piece, right_piece, ssem.at[23], share_recv.at[1, d],
-                dev(x, add(y, d, N), z, k),
-            ).start()
-
-        loop(1, N, share_r)
-
-    loop(0, N, forward)
+    def forward_half(h):
+        rows = rank_halves[h]
+
+        def forward(i):
+            b, c = add(y, i, N), add(z, i, N)
+            left_piece = rbl.at[z, rows, span(b, hc)]
+            right_piece = rbr.at[y, rows, span(c, hc)]
+            bytes_wait(left_piece, piece_recv.at[0, h, b])
+
+            def share_l(d):
+                remote(
+                    left_piece, left_piece, ssem.at[22], share_recv.at[0, d],
+                    dev(x, y, add(z, d, N), k),
+                ).start()
+
+            loop(1, N, share_l)
+            bytes_wait(right_piece, piece_recv.at[1, h, c])
+
+            def share_r(d):
+                remote(
+                    right_piece, right_piece, ssem.at[23], share_recv.at[1, d],
+                    dev(x, add(y, d, N), z, k),
+                ).start()
+
+            loop(1, N, share_r)
+
+        loop(0, N, forward)
+
+    forward_half(0)
+    forward_half(1)
     later(rbl.at[part3], ssem.at[22])
     later(rbr.at[part3], ssem.at[23])
 
@@ -817,7 +856,9 @@
             pltpu.SemaphoreType.DMA((3, 4)),
             pltpu.SemaphoreType.DMA((3, 4)),
             pltpu.SemaphoreType.DMA((2, N)),
-            pltpu.SemaphoreType.DMA((2, N)),
+            pltpu.SemaphoreType.DMA((2, 2, N)),
+            pltpu.SemaphoreType.DMA((6, 2)),
+            pltpu.SemaphoreType.DMA((6, 2)),
         ],
         compiler_params=pltpu.CompilerParams(
             collective_id=0, has_side_effects=True, vmem_limit_bytes=60 * 1024 * 1024

time: 302 us -> 293 us (0.970)
  Pallas kernels: 298 us -> 289 us
    pallas_call x1, Pallas kernels: 298 us -> 289 us  [owners(): pl.pallas_call(functools.partial(body, float(width) ** 0.5), out_shape=ja...]
where the time goes in v7:
time: 293 us
  Pallas kernels  289 us (99%)
  local copies, waits for them, and re-layouts  3.86 us (1%)
    pallas_call x1, Pallas kernels, owners(): pl.pallas_call(functools.partial(body, float(width) ** 0.5), out_shape=ja...  289 us

profile of v7, /device:TPU:0, one launch (start us, length us, event | category | flops | bytes accessed | tf_op | source)
XLA Modules:
  0.0 292.6 jit_solution(8280837430245133613)
XLA Ops:
  0.0 0.8 copy.7
  0.8 0.7 reshape.6.row_ids
  1.5 0.7 reshape_reshape.4.col_ids
  2.2 288.7 %owners.1 = f32[1,384,128]{2,1,0:T(8,128)} custom-call(s32[1,256]{1,0:T(1,128)} %reshape.6.row_ids, s32[256,1]{1,0:T(8,128)} %reshape_reshape.4.col_ids, bf16[128,2,16384]{2,1,0:T(2,128)(2,1)} %grads.1, bf16[128,6144]{1,0:T(8,128)(2,1)} %acts.1, bf16[16384,128]{1,0:T(8,128)(2,1)} %bitcast.1), custom_call_target="tpu_custom_call" | custom-call | tf_op jit(solution)/shard_map/owners/pallas_call | solution.py:827
  291.0 1.6 copy.11

commit v8 on v7

--- a/solution.py
+++ b/solution.py
@@ -32,24 +32,30 @@
     )
 
 
-def picks(row_ids, col_ids, pick, pick_x):
-    pairs = row_ids.shape[1]
+def picks(ids_ref, pick, pick_x):
     toks = pick_x.shape[1]
-    top = pairs // toks
-    ids = row_ids[...]
-    same = (col_ids[...] == ids) & (
-        lax.broadcasted_iota(jnp.int32, (pairs, pairs), 0)
-        < lax.broadcasted_iota(jnp.int32, (pairs, pairs), 1)
-    )
-    rank = jnp.sum(same.astype(F32), axis=0, keepdims=True).astype(jnp.int32)
-    slot = ids * CAP + rank
-    hot = lax.broadcasted_iota(jnp.int32, (ROWS, pairs), 0) == slot
-    pick[...] = hot.astype(F32).astype(BF16)
-    token = lax.broadcasted_iota(jnp.int32, (pairs, toks), 0) - top * lax.broadcasted_iota(
-        jnp.int32, (pairs, toks), 1
-    )
-    of_token = ((token >= 0) & (token < top)).astype(F32).astype(BF16)
-    pick_x[...] = dot(pick[...], of_token).astype(BF16)
+    top = pick.shape[1] // toks
+    ids = ids_ref[...].astype(F32)
+    q = lax.broadcasted_iota(jnp.int32, (toks, toks), 0)
+    p = lax.broadcasted_iota(jnp.int32, (toks, toks), 1)
+    slot_row = lax.broadcasted_iota(jnp.int32, (ROWS, toks), 0).astype(F32)
+    token = lax.broadcasted_iota(jnp.int32, (toks, top * toks), 0) * top
+    pair = lax.broadcasted_iota(jnp.int32, (toks, top * toks), 1)
+    along = [jnp.broadcast_to(ids[i : i + 1, :], (toks, toks)) for i in range(top)]
+    down = [v.T for v in along]
+    placed = jnp.zeros(pick.shape, F32)
+    by_token = jnp.zeros(pick_x.shape, F32)
+    for i in range(top):
+        ahead = ((down[i] == along[i]) & (q < p)).astype(F32)
+        for j in range(i):
+            ahead = ahead + (down[j] == along[i]).astype(F32)
+        slot = ids[i : i + 1, :] * CAP + jnp.sum(ahead, axis=0, keepdims=True)
+        hot = (slot_row == slot).astype(F32)
+        by_token = by_token + hot
+        spread = (pair == token + i).astype(F32).astype(BF16)
+        placed = placed + dot(hot.astype(BF16), spread)
+    pick[...] = placed.astype(BF16)
+    pick_x[...] = by_token.astype(BF16)
 
 
 def bytes_wait(ref, sem):
@@ -104,7 +110,7 @@
 
 def body(
     scale,
-    row_ids, col_ids, grads, acts, om,
+    ids_ref, grads, acts, om,
     out,
     pick, pick_x, g_in, gs, xs,
     xr, gl, gr, wl, wr,
@@ -194,7 +200,7 @@
         greet(dev(x, y, add(z, d, N), 1 - k))
 
     loop(1, N, other_core_y)
-    picks(row_ids, col_ids, pick, pick_x)
+    picks(ids_ref, pick, pick_x)
     part = pl.ds(0, ROWS - CAP)
 
     def sort_side(i, side, first):
@@ -397,8 +403,14 @@
 
         return total
 
+    rh = RANK // 2
+    gram_lane = lax.broadcasted_iota(jnp.int32, (rh // 2, RANK), 1)
+
     def gram_all(s, phase):
-        gm[phase] = dot_t(s, s, HIGH).astype(BF16)
+        gram = dot_t(s, s, HIGH)
+        fold = pltpu.roll(gram[rh : rh + rh // 2], rh, 1)
+        low = jnp.where(gram_lane < rh, fold, gram[rh + rh // 2 :])
+        gm[phase] = jnp.concatenate([gram[:rh], low], axis=0).astype(BF16)
         pltpu.make_async_copy(gm.at[phase], gb.at[phase, tok], gsem.at[2 * phase]).start()
 
         def go(d):
@@ -410,10 +422,13 @@
         loop(1, TOK, go)
         bytes_wait(gb.at[phase], gsem.at[2 * phase])
         c = lax.fori_loop(
-            0, TOK, lambda i, c: c + gb[phase, i].astype(F32), jnp.zeros((RANK, RANK), F32)
+            0, TOK, lambda i, c: c + gb[phase, i].astype(F32), jnp.zeros((RANK - rh // 2, RANK), F32)
         )
         bytes_wait(gb.at[phase, pl.ds(0, TOK - 1)], gsem.at[2 * phase + 1])
-        return inverse_factor(c, cm, mm)
+        low = c[rh:]
+        upper = jnp.where(gram_lane < rh, 0.0, pltpu.roll(low, rh, 1))
+        lower = jnp.where(gram_lane < rh, 0.0, low)
+        return inverse_factor(jnp.concatenate([c[:rh], upper, lower], axis=0), cm, mm)
 
     part3 = pl.ds(0, N - 1)
 
@@ -433,8 +448,6 @@
         return pl.ds(pl.multiple_of(i * n, 128), n)
 
     wg, hg = N * wc, N * hc
-
-    rh = RANK // 2
 
     def reduce_x(p, phase):
         pt = p.T.astype(BF16)
@@ -812,7 +825,7 @@
         drain()
 
 
-def owners(row_ids, col_ids, grads, acts, om):
+def owners(ids, grads, acts, om):
     toks, top, hidden = grads.shape
     width = acts.shape[1]
     half = hidden // 2
@@ -827,7 +840,7 @@
     return pl.pallas_call(
         functools.partial(body, float(width) ** 0.5),
         out_shape=jax.ShapeDtypeStruct((1, wc, RANK), F32),
-        in_specs=[pl.BlockSpec(memory_space=pltpu.VMEM)] * 2 + [any_spec] * 3,
+        in_specs=[pl.BlockSpec(memory_space=pltpu.VMEM)] + [any_spec] * 3,
         out_specs=pl.BlockSpec(memory_space=pltpu.VMEM),
         scratch_shapes=[
             vm(ROWS, toks * top), vm(ROWS, toks), vm(2, 2, toks, top, chunk),
@@ -843,7 +856,7 @@
             vm(N, RANK, hc), vm(N, RANK, hc), vm(N, RANK, hc), vm(N, RANK, hc),
             vm(N, RANK, hc), vm(N, RANK, hc),
             vm(RANK, hc), vm(RANK, hc), vm(N, RANK, N * hc), vm(N, RANK, N * hc),
-            vm(3, RANK, RANK), vm(3, TOK, RANK, RANK),
+            vm(3, RANK - rh // 2, RANK), vm(3, TOK, RANK - rh // 2, RANK),
             vm(RANK, RANK, dtype=F32), vm(RANK, RANK, dtype=F32),
             pltpu.SemaphoreType.DMA((24,)),
             pltpu.SemaphoreType.DMA((26,)),
@@ -864,13 +877,12 @@
             collective_id=0, has_side_effects=True, vmem_limit_bytes=60 * 1024 * 1024
         ),
         name="owners",
-    )(row_ids, col_ids, grads, acts, om)
+    )(ids, grads, acts, om)
 
 
 def shards(activations, expert_ids, out_grads, sketch_matrix):
-    ids = expert_ids.reshape(1, -1)
     om = sketch_matrix.reshape(sketch_matrix.shape[1:])
-    return owners(ids, ids.reshape(-1, 1), out_grads, activations, om)
+    return owners(expert_ids.T, out_grads, activations, om)
 
 
 def solution(mesh):

time: 293 us -> 286 us (0.976)
  Pallas kernels: 289 us -> 284 us
    pallas_call x1, Pallas kernels: 289 us -> 284 us  [owners(): pl.pallas_call(functools.partial(body, float(width) ** 0.5), out_shape=ja...]
where the time goes in v8:
time: 286 us
  Pallas kernels  284 us (99%)
    pallas_call x1, Pallas kernels, owners(): pl.pallas_call(functools.partial(body, float(width) ** 0.5), out_shape=ja...  284 us

profile of v8, /device:TPU:0, one launch (start us, length us, event | category | flops | bytes accessed | tf_op | source)
XLA Modules:
  0.0 285.6 jit_solution(8193214050238317787)
XLA Ops:
  0.0 283.9 %owners.1 = f32[1,384,128]{2,1,0:T(8,128)} custom-call(s32[2,128]{1,0:T(2,128)} %bitcast.3, bf16[128,2,16384]{2,1,0:T(2,128)(2,1)} %grads.1, bf16[128,6144]{1,0:T(8,128)(2,1)} %acts.1, bf16[16384,128]{1,0:T(8,128)(2,1)} %bitcast.2), custom_call_target="tpu_custom_call" | custom-call | tf_op jit(solution)/shard_map/owners/pallas_call | solution.py:840
  284.0 1.6 copy.6

commit v9 on v8

--- a/solution.py
+++ b/solution.py
@@ -117,10 +117,10 @@
     nls, nrs, pxl, pxr, pxl2, pxr2,
     spa, spb, ra1, rb1, mid_a, mid_b, ra2, rb2, bta, btb,
     ws, wgl, wgr,
-    pwl, pwr, rl1, rr1, mid_l, mid_r, turn_l, turn_r, rl2, rr2, own_rl, own_rr, rbl, rbr,
+    pwl, pwr, rl1, rr1, turn_l, turn_r, rl2, rr2, own_rl, own_rr, rbl, rbr,
     gm, gb, cm, mm,
     ssem, rsem, gsem, selfsem, in_sem, slot_sem, left_sem, right_sem,
-    line_send, line_recv, share_recv, piece_recv, half_send, half_recv,
+    line_send, line_recv, share_recv, piece_recv, half_send, half_recv, om_recv,
 ):
     tok = lax.axis_index("tok")
     ex = lax.axis_index("exp")
@@ -325,21 +325,29 @@
     bytes_wait(wl.at[om_rows(z), :], rsem.at[0])
     bytes_wait(wr.at[om_rows(y), :], rsem.at[1])
 
-    def om_share(d):
-        remote(
-            wl.at[om_rows(z), :], wl.at[om_rows(z), :], ssem.at[18], rsem.at[18],
-            dev(x, y, add(z, d, N), k),
-        ).start()
-        remote(
-            wr.at[om_rows(y), :], wr.at[om_rows(y), :], ssem.at[19], rsem.at[19],
-            dev(x, add(y, d, N), z, k),
-        ).start()
-
-    loop(1, N, om_share)
-    most = pl.ds(0, 3 * quarter)
-    later(wl.at[most, :], ssem.at[18])
-    later(wr.at[most, :], ssem.at[19])
-    loop(chunks // 2, chunks, lambda i: send_chunk(i, False))
+    def line(side, d):
+        return dev(x, y, add(z, d, N), k) if side == 0 else dev(x, add(y, d, N), z, k)
+
+    sides = ((0, wl, z), (1, wr, y))
+    for side, buf, me in sides:
+        mine = buf.at[om_rows(me), :]
+        remote(mine, mine, ssem.at[18 + side], om_recv.at[side, 0], line(side, 1)).start()
+        remote(mine, mine, ssem.at[18 + side], om_recv.at[side, 1], line(side, N - 1)).start()
+        later(buf.at[pl.ds(0, 2 * quarter), :], ssem.at[18 + side])
+
+    loop(chunks // 2, chunks - 1, lambda i: send_chunk(i, False))
+    short = quarter // 2
+    for side, buf, me in sides:
+        below, above = add(me, N - 1, N), add(me, 1, N)
+        bytes_wait(buf.at[om_rows(below), :], om_recv.at[side, 0])
+        low = buf.at[pl.ds(pl.multiple_of(below * quarter, quarter), short), :]
+        remote(low, low, ssem.at[24 + side], om_recv.at[side, 2], line(side, 1)).start()
+        bytes_wait(buf.at[om_rows(above), :], om_recv.at[side, 1])
+        high = buf.at[pl.ds(pl.multiple_of(above * quarter + short, short), short), :]
+        remote(high, high, ssem.at[24 + side], om_recv.at[side, 2], line(side, N - 1)).start()
+        later(buf.at[pl.ds(0, quarter), :], ssem.at[24 + side])
+
+    send_chunk(chunks - 1, False)
     for slot in range(2):
         later(gs.at[0, slot, part, :], slot_sem.at[0, slot])
         later(gs.at[1, slot, part, :], slot_sem.at[1, slot])
@@ -505,8 +513,9 @@
         bytes_wait(mid_b.at[part3], s.at[3])
         return jnp.concatenate([top, low], axis=0)
 
-    bytes_wait(wl.at[most, :], rsem.at[18])
-    bytes_wait(wr.at[most, :], rsem.at[19])
+    for side, buf, me in sides:
+        bytes_wait(buf.at[om_rows(add(me, 2, N)), :], om_recv.at[side, 2])
+
 
     def proj_chunk(i, acc):
         cols = pl.ds(pl.multiple_of(i * chunk, chunk), chunk)
@@ -663,30 +672,32 @@
 
         def stage2_left(i):
             b = add(y, i, N)
-            mid_l[b, rows] = sum_along(pwl, rl1, z, span(b, hc), rows).astype(BF16)
+            pwl[z, rows, span(b, hc)] = sum_along(pwl, rl1, z, span(b, hc), rows).astype(BF16)
 
             @pl.when(i < N)
             def _():
                 remote(
-                    mid_l.at[b, rows], turn_l.at[y, rows], s_h[2], r_h[2], dev(x, b, z, k)
+                    pwl.at[z, rows, span(b, hc)], turn_l.at[y, rows], s_h[2], r_h[2],
+                    dev(x, b, z, k),
                 ).start()
 
         def stage2_right(i):
             c = add(z, i, N)
-            mid_r[c, rows] = sum_along(pwr, rr1, y, span(c, hc), rows).astype(BF16)
+            pwr[y, rows, span(c, hc)] = sum_along(pwr, rr1, y, span(c, hc), rows).astype(BF16)
 
             @pl.when(i < N)
             def _():
                 remote(
-                    mid_r.at[c, rows], turn_r.at[z, rows], s_h[3], r_h[3], dev(x, y, c, k)
+                    pwr.at[y, rows, span(c, hc)], turn_r.at[z, rows], s_h[3], r_h[3],
+                    dev(x, y, c, k),
                 ).start()
 
         bytes_wait(rl1.at[part3, rows], r_h[0])
         loop(1, N + 1, stage2_left)
-        turn_l[y, rows] = mid_l[y, rows]
+        turn_l[y, rows] = pwl[z, rows, span(y, hc)]
         bytes_wait(rr1.at[part3, rows], r_h[1])
         loop(1, N + 1, stage2_right)
-        turn_r[z, rows] = mid_r[z, rows]
+        turn_r[z, rows] = pwr[y, rows, span(z, hc)]
 
         def along_x_left(i):
             remote(
@@ -704,8 +715,8 @@
         bytes_wait(turn_r.at[part3, rows], r_h[3])
         loop(1, N, along_x_right)
         rr2[x, rows] = turn_r[0, rows]
-        later(mid_l.at[part3, rows], s_h[2])
-        later(mid_r.at[part3, rows], s_h[3])
+        later(turn_l.at[part3, rows], s_h[2])
+        later(turn_r.at[part3, rows], s_h[3])
         later(rl2.at[part3, rows], s_h[4])
         later(rr2.at[part3, rows], s_h[5])
 
@@ -769,29 +780,37 @@
             right_piece = rbr.at[y, rows, span(c, hc)]
             bytes_wait(left_piece, piece_recv.at[0, h, b])
 
-            def share_l(d):
+            for turn, d in enumerate((1, N - 1)):
                 remote(
-                    left_piece, left_piece, ssem.at[22], share_recv.at[0, d],
-                    dev(x, y, add(z, d, N), k),
+                    left_piece, left_piece, ssem.at[22], share_recv.at[0, turn, h], line(0, d)
                 ).start()
 
-            loop(1, N, share_l)
             bytes_wait(right_piece, piece_recv.at[1, h, c])
 
-            def share_r(d):
+            for turn, d in enumerate((1, N - 1)):
                 remote(
-                    right_piece, right_piece, ssem.at[23], share_recv.at[1, d],
-                    dev(x, add(y, d, N), z, k),
+                    right_piece, right_piece, ssem.at[23], share_recv.at[1, turn, h], line(1, d)
                 ).start()
-
-            loop(1, N, share_r)
 
         loop(0, N, forward)
 
     forward_half(0)
     forward_half(1)
-    later(rbl.at[part3], ssem.at[22])
-    later(rbr.at[part3], ssem.at[23])
+    pair2 = pl.ds(0, 2)
+    later(rbl.at[pair2], ssem.at[22])
+    later(rbr.at[pair2], ssem.at[23])
+
+    groups = ((0, rbl, z), (1, rbr, y))
+    for h, turn, back, d in ((0, 0, N - 1, 1), (1, 1, 1, N - 1)):
+        for side, buf, me in groups:
+            rows_h = buf.at[add(me, back, N), rank_halves[h]]
+            bytes_wait(rows_h, share_recv.at[side, turn, h])
+            remote(
+                rows_h, rows_h, ssem.at[26 + side], share_recv.at[side, 2, h], line(side, d)
+            ).start()
+
+    later(rbl.at[0], ssem.at[26])
+    later(rbr.at[0], ssem.at[27])
 
     def left_group(g, acc):
         return acc + dot_t(gl[:, span(g, hg)], rbl[g])
@@ -803,17 +822,19 @@
     left = left_group(z, zero)
     right = right_group(y, zero)
 
-    def next_groups(d, acc):
-        a, b = acc
-        g = add(z, N - d, N)
-        bytes_wait(rbl.at[g], share_recv.at[0, d])
-        a = left_group(g, a)
-        g = add(y, N - d, N)
-        bytes_wait(rbr.at[g], share_recv.at[1, d])
-        b = right_group(g, b)
-        return a, b
-
-    left, right = lax.fori_loop(1, N, next_groups, (left, right))
+    for turn, back in ((0, N - 1), (1, 1)):
+        g, g2 = add(z, back, N), add(y, back, N)
+        bytes_wait(rbl.at[g, rank_halves[1 - turn]], share_recv.at[0, turn, 1 - turn])
+        left = left_group(g, left)
+        bytes_wait(rbr.at[g2, rank_halves[1 - turn]], share_recv.at[1, turn, 1 - turn])
+        right = right_group(g2, right)
+
+    g, g2 = add(z, 2, N), add(y, 2, N)
+    for h in range(2):
+        bytes_wait(rbl.at[g, rank_halves[h]], share_recv.at[0, 2, h])
+        bytes_wait(rbr.at[g2, rank_halves[h]], share_recv.at[1, 2, h])
+    left = left_group(g, left)
+    right = right_group(g2, right)
     second = to_x(left, right, pxl2, pxr2, 1).astype(BF16).astype(F32)
 
     s3 = reduce_x(second, 1)
@@ -854,11 +875,10 @@
             vm(ROWS, RANK), vm(ROWS, RANK), vm(ROWS, RANK),
             vm(N, RANK, N * hc), vm(N, RANK, N * hc), vm(N, RANK, N * hc), vm(N, RANK, N * hc),
             vm(N, RANK, hc), vm(N, RANK, hc), vm(N, RANK, hc), vm(N, RANK, hc),
-            vm(N, RANK, hc), vm(N, RANK, hc),
             vm(RANK, hc), vm(RANK, hc), vm(N, RANK, N * hc), vm(N, RANK, N * hc),
             vm(3, RANK - rh // 2, RANK), vm(3, TOK, RANK - rh // 2, RANK),
             vm(RANK, RANK, dtype=F32), vm(RANK, RANK, dtype=F32),
-            pltpu.SemaphoreType.DMA((24,)),
+            pltpu.SemaphoreType.DMA((28,)),
             pltpu.SemaphoreType.DMA((26,)),
             pltpu.SemaphoreType.DMA((6,)),
             pltpu.SemaphoreType.DMA((18,)),
@@ -868,10 +888,11 @@
             pltpu.SemaphoreType.DMA((8,)),
             pltpu.SemaphoreType.DMA((3, 4)),
             pltpu.SemaphoreType.DMA((3, 4)),
-            pltpu.SemaphoreType.DMA((2, N)),
+            pltpu.SemaphoreType.DMA((2, 3, 2)),
             pltpu.SemaphoreType.DMA((2, 2, N)),
             pltpu.SemaphoreType.DMA((6, 2)),
             pltpu.SemaphoreType.DMA((6, 2)),
+            pltpu.SemaphoreType.DMA((2, 3)),
         ],
         compiler_params=pltpu.CompilerParams(
             collective_id=0, has_side_effects=True, vmem_limit_bytes=60 * 1024 * 1024

time: 286 us -> 273 us (0.955)
  Pallas kernels: 284 us -> 272 us
    pallas_call x1, Pallas kernels: 284 us -> 272 us  [owners(): pl.pallas_call(functools.partial(body, float(width) ** 0.5), out_shape=ja...]
where the time goes in v9:
time: 273 us
  Pallas kernels  272 us (100%)
    pallas_call x1, Pallas kernels, owners(): pl.pallas_call(functools.partial(body, float(width) ** 0.5), out_shape=ja...  272 us

profile of v9, /device:TPU:0, one launch (start us, length us, event | category | flops | bytes accessed | tf_op | source)
XLA Modules:
  0.0 273.3 jit_solution(10549217362897645326)
XLA Ops:
  0.0 271.6 %owners.1 = f32[1,384,128]{2,1,0:T(8,128)} custom-call(s32[2,128]{1,0:T(2,128)} %bitcast.3, bf16[128,2,16384]{2,1,0:T(2,128)(2,1)} %grads.1, bf16[128,6144]{1,0:T(8,128)(2,1)} %acts.1, bf16[16384,128]{1,0:T(8,128)(2,1)} %bitcast.2), custom_call_target="tpu_custom_call" | custom-call | tf_op jit(solution)/shard_map/owners/pallas_call | solution.py:861
  271.6 1.6 copy.6

commit v10 on v9

--- a/solution.py
+++ b/solution.py
@@ -182,13 +182,19 @@
     def greet(where):
         pl.semaphore_signal(barrier, inc=1, device_id=where, device_id_type=MESH)
 
-    chip = x * TOK + tok
+    def same_experts(d):
+        greet((add(tok, d, TOK), ex))
+
+    loop(1, TOK, same_experts)
 
     def same_core(d):
-        c = add(chip, d, N * TOK)
-        greet((lax.rem(c, TOK), lax.div(c, TOK) * 2 + k))
-
-    loop(1, N * TOK, same_core)
+        greet(dev(add(x, d, N), y, z, k))
+        greet(dev(add(x, y, N), add(y, d, N), z, k))
+        greet(dev(add(x, N - z, N), y, add(z, d, N), k))
+        greet(dev(add(x + N - y, d, N), add(y, N - d, N), z, k))
+        greet(dev(add(x + z, d, N), y, add(z, d, N), k))
+
+    loop(1, N, same_core)
 
     def other_core(d):
         greet(dev(add(x, d, N), y, z, 1 - k))
@@ -217,7 +223,7 @@
 
     sort_side(0, 0, True)
     sort_side(0, 1, True)
-    pl.semaphore_wait(barrier, N * TOK - 1 + N + 2 * (N - 1))
+    pl.semaphore_wait(barrier, TOK - 1 + 5 * (N - 1) + N + 2 * (N - 1))
 
     shift_r = lax.rem(N - z, N)
     swap_l = y == 0
@@ -549,21 +555,31 @@
         ).start()
 
     loop(1, N, first_b)
+    def then_a(i):
+        piece_a = bta.at[y, :, span(add(z, i, N), wc)]
+
+        def go(d):
+            remote(
+                piece_a, piece_a, line_send.at[2, 2], line_recv.at[2, 2], dev(x, add(y, d, N), z, k)
+            ).start()
+
+        loop(1, N, go)
+
+    def then_b(i):
+        piece_b = btb.at[z, :, span(add(y, i, N), wc)]
+
+        def go(d):
+            remote(
+                piece_b, piece_b, line_send.at[2, 3], line_recv.at[2, 3], dev(x, y, add(z, d, N), k)
+            ).start()
+
+        loop(1, N, go)
+
+    then_a(0)
+    then_b(0)
     bytes_wait(bta.at[y, :, three], line_recv.at[2, 0])
-
-    def then_a(d):
-        remote(
-            bta.at[y], bta.at[y], line_send.at[2, 2], line_recv.at[2, 2], dev(x, add(y, d, N), z, k)
-        ).start()
-
     loop(1, N, then_a)
     bytes_wait(btb.at[z, :, three], line_recv.at[2, 1])
-
-    def then_b(d):
-        remote(
-            btb.at[z], btb.at[z], line_send.at[2, 3], line_recv.at[2, 3], dev(x, y, add(z, d, N), k)
-        ).start()
-
     loop(1, N, then_b)
     later(bta.at[0, :, three], line_send.at[2, 0])
     later(btb.at[0, :, three], line_send.at[2, 1])

time: 273 us -> 265 us (0.971)
  Pallas kernels: 272 us -> 263 us
    pallas_call x1, Pallas kernels: 272 us -> 263 us  [owners(): pl.pallas_call(functools.partial(body, float(width) ** 0.5), out_shape=ja...]
where the time goes in v10:
time: 265 us
  Pallas kernels  263 us (99%)
    pallas_call x1, Pallas kernels, owners(): pl.pallas_call(functools.partial(body, float(width) ** 0.5), out_shape=ja...  263 us

profile of v10, /device:TPU:0, one launch (start us, length us, event | category | flops | bytes accessed | tf_op | source)
XLA Modules:
  0.0 264.9 jit_solution(12761143411133018414)
XLA Ops:
  0.0 263.3 %owners.1 = f32[1,384,128]{2,1,0:T(8,128)} custom-call(s32[2,128]{1,0:T(2,128)} %bitcast.3, bf16[128,2,16384]{2,1,0:T(2,128)(2,1)} %grads.1, bf16[128,6144]{1,0:T(8,128)(2,1)} %acts.1, bf16[16384,128]{1,0:T(8,128)(2,1)} %bitcast.2), custom_call_target="tpu_custom_call" | custom-call | tf_op jit(solution)/shard_map/owners/pallas_call | solution.py:877
  263.3 1.6 copy.6

commit v11 on v10

--- a/solution.py
+++ b/solution.py
@@ -327,7 +327,7 @@
     pltpu.make_async_copy(xs.at[rows_of(ex), :], xr.at[rows_of(ex), :], rsem.at[4]).start()
 
     send_chunk(1, True)
-    loop(2, chunks // 2, lambda i: send_chunk(i, False))
+    loop(2, 3, lambda i: send_chunk(i, False))
     bytes_wait(wl.at[om_rows(z), :], rsem.at[0])
     bytes_wait(wr.at[om_rows(y), :], rsem.at[1])
 
@@ -341,7 +341,7 @@
         remote(mine, mine, ssem.at[18 + side], om_recv.at[side, 1], line(side, N - 1)).start()
         later(buf.at[pl.ds(0, 2 * quarter), :], ssem.at[18 + side])
 
-    loop(chunks // 2, chunks - 1, lambda i: send_chunk(i, False))
+    loop(3, chunks - 1, lambda i: send_chunk(i, False))
     short = quarter // 2
     for side, buf, me in sides:
         below, above = add(me, N - 1, N), add(me, 1, N)

time: 265 us -> 267 us (level)
  no operation moved by 1% of the time
where the time goes in v11:
time: 267 us; the launch traced here: 266 us
  Pallas kernels  265 us (99%)
    pallas_call x1, Pallas kernels, owners(): pl.pallas_call(functools.partial(body, float(width) ** 0.5), out_shape=ja...  265 us

profile of v11, /device:TPU:0, one launch (start us, length us, event | category | flops | bytes accessed | tf_op | source)
XLA Modules:
  0.0 266.4 jit_solution(10792062347454617228)
XLA Ops:
  0.0 264.8 %owners.1 = f32[1,384,128]{2,1,0:T(8,128)} custom-call(s32[2,128]{1,0:T(2,128)} %bitcast.3, bf16[128,2,16384]{2,1,0:T(2,128)(2,1)} %grads.1, bf16[128,6144]{1,0:T(8,128)(2,1)} %acts.1, bf16[16384,128]{1,0:T(8,128)(2,1)} %bitcast.2), custom_call_target="tpu_custom_call" | custom-call | tf_op jit(solution)/shard_map/owners/pallas_call | solution.py:877
  264.8 1.6 copy.6
